TPU v7x, 128 devices: a whole 4x4x4 slice. The times are simulated.
128 devices in a mesh: gx: 16 (over x, y), gy: 4 (over z), gz: 2 (over core).
Axes of the slice: x: 4, y: 4, z: 4, core: 2. Of those that a mesh axis runs over, the one named last changes fastest.
Arguments:
- thermal_state: float32 [512, 512, 256], P('gx', 'gy', 'gz'), may hold values from -12 to 12
- material_kinds: int32 [512, 512, 256], P('gx', 'gy', 'gz'), may hold values from 0 to 7
- axial_diffusivity_by_kind: float32 [8], replicated, may hold values from 1000 to 8000
- crosswise_diffusivity_by_kind: float32 [2, 8], replicated, may hold values from 0.04 to 0.2
Outputs:
- new_temperature: float32 [512, 512, 256], P('gx', 'gy', 'gz')
Inputs may be any that keep to these rules, and one draw needn't show every extreme that they name: `material_kinds`: indexes the tables' last dimension.
All inputs are finite; a program needn't handle non-finite values.
Results may differ from a plain program's by a relative error of at most 0.0003.
Values sent between devices are 32-bit elements; how exact they have to be, the bound alone decides.
No kernel may reach another device: no remote copies, remote signals or barrier semaphores. Data moves between devices by JAX's collectives and lax.ppermute only.
A program may use at most 128 MiB of HBM per device.

v0:
```python
import functools

import jax
import jax.numpy as jnp
from jax import lax
from jax.experimental import pallas as pl
from jax.experimental.pallas import tpu as pltpu
from jax.sharding import PartitionSpec as P

F32 = jnp.float32
LANES = 128
GROUP = 8
VMEM_LIMIT = 8 * 1024 * 1024
CHUNKS = 4
BLOCK = 8
SMEM_SPEC = pl.BlockSpec(memory_space=pltpu.SMEM)
VMEM_SPEC = pl.BlockSpec(memory_space=pltpu.VMEM)
ANY_SPEC = pl.BlockSpec(memory_space=pl.ANY)


def iota(shape, axis):
    return lax.broadcasted_iota(jnp.int32, shape, axis)


def half_table(table, row, classes):
    return [(table[c] if row is None else table[row, c]) * 0.5 for c in range(classes)]


def masks(kinds):
    return kinds >= 4, (kinds & 2) != 0, (kinds & 1) != 0


def choose(table, bits):
    level = list(table)
    for bit in bits:
        half = len(level) // 2
        level = [jnp.where(bit, high, low) for low, high in zip(level[:half], level[half:])]
    return level[0]


def pick(table, kinds):
    return choose(table, masks(kinds))


def pick_two(first, second, kinds):
    bits = masks(kinds)
    return choose(first, bits), choose(second, bits)


def reciprocal(x):
    r = pl.reciprocal(x, approx=True)
    return r * (2.0 - x * r)


def faces_kernel(nx, ny, cross, u_hbm, kind_hbm, u_ref, kind_ref, ya_ref, yb_ref, z_ref, k_pack, sems):
    step = nx // CHUNKS
    copies = []
    for c in range(CHUNKS):
        part = pl.ds(c * step, step)
        pair = (
            pltpu.make_async_copy(u_hbm.at[part], u_ref.at[part], sems.at[0, c]),
            pltpu.make_async_copy(kind_hbm.at[part], kind_ref.at[part], sems.at[1, c]),
        )
        for copy in pair:
            copy.start()
        copies.append(pair)
    classes = cross.shape[1]
    ky = half_table(cross, 0, classes)
    kz = half_table(cross, 1, classes)
    even = lax.axis_index("gy") % 2 == 0
    inner = jnp.where(lax.axis_index("gz") == 0, LANES - 1, 0)
    lane = iota((GROUP, LANES), 1)
    for c in range(CHUNKS):
        for copy in copies[c]:
            copy.wait()
        for g in range(ny // GROUP):
            rows = pl.ds(g * GROUP, GROUP)
            u_pack = jnp.zeros((GROUP, LANES), F32) if c == 0 else z_ref[rows]
            kinds = jnp.zeros((GROUP, LANES), jnp.int32) if c == 0 else k_pack[rows]
            for i in range(c * step, (c + 1) * step):
                shift = lax.rem(LANES + i - inner, LANES)
                u_pack = jnp.where(lane == i, pltpu.roll(u_ref[i, rows], shift, 1), u_pack)
                kinds = jnp.where(lane == i, pltpu.roll(kind_ref[i, rows], shift, 1), kinds)
            if c < CHUNKS - 1:
                z_ref[rows], k_pack[rows] = u_pack, kinds
            else:
                hz = pltpu.roll(pick(kz, kinds), nx, 1)
                z_ref[rows] = jnp.where(lane < nx, u_pack, hz)
    u_top, u_bottom = u_ref[:, ny - 1, :], u_ref[:, 0, :]
    k_top, k_bottom = pick(ky, kind_ref[:, ny - 1, :]), pick(ky, kind_ref[:, 0, :])
    ya_ref[0] = jnp.where(even, u_top, u_bottom)
    ya_ref[1] = jnp.where(even, k_top, k_bottom)
    yb_ref[0] = jnp.where(even, u_bottom, u_top)
    yb_ref[1] = jnp.where(even, k_bottom, k_top)


def source_kernel(nx, ny, cross, u_ref, kind_ref, s_ref):
    classes = cross.shape[1]
    ky = half_table(cross, 0, classes)
    kz = half_table(cross, 1, classes)
    core = lax.axis_index("gz")
    lane = iota((GROUP, LANES), 1)
    row = iota((GROUP, LANES), 0)
    last_lane = lane == LANES - 1
    outer = lane == jnp.where(core == 0, 0, LANES - 1)
    groups = ny // GROUP

    for i in range(nx):
        def fetch(g):
            u = u_ref[i, pl.ds(g * GROUP, GROUP)]
            hy, hz = pick_two(ky, kz, kind_ref[i, pl.ds(g * GROUP, GROUP)])
            return u, hz, hy, pltpu.roll(u, GROUP - 1, 0), pltpu.roll(hy, GROUP - 1, 0)

        now = fetch(0)
        below = jnp.zeros((GROUP, LANES), F32)
        for g in range(groups):
            u, hz, hy, u_rolled, hy_rolled = now
            if g < groups - 1:
                now = fetch(g + 1)
                u_up = jnp.where(row == GROUP - 1, now[3], u_rolled)
                hy_up = jnp.where(row == GROUP - 1, now[4], hy_rolled)
                flux = (hy + hy_up) * (u_up - u)
            else:
                flux = jnp.where(row == GROUP - 1, 0.0, (hy + hy_rolled) * (u_rolled - u))
            down = pltpu.roll(flux, 1, 0)
            total = u + flux - jnp.where(row == 0, below, down)
            below = down
            z_flux = (hz + pltpu.roll(hz, LANES - 1, 1)) * (pltpu.roll(u, LANES - 1, 1) - u)
            z_down = (hz + pltpu.roll(hz, 1, 1)) * (u - pltpu.roll(u, 1, 1))
            total = total + (jnp.where(last_lane, 0.0, z_flux) - jnp.where(lane == 0, 0.0, z_down))
            s_ref[i, pl.ds(g * GROUP, GROUP)] = jnp.where(outer, total - hz * u, total)


def sweep_kernel(
    nx, ny, axial, ya, yb, z, ya_in, yb_in, z_in, kind_ref, s_ref, t_ref, e_ref, q_ref, send_ref, top, bottom
):
    at, last = lax.axis_index("gy"), lax.axis_size("gy") - 1
    even = at % 2 == 0
    core = lax.axis_index("gz")

    def edge(own, other, inside):
        keep = jnp.where(inside, 1.0, 0.0)
        return (own[1] + other[1] * keep) * (other[0] * keep - own[0])

    has_up, has_down = at < last, at > 0
    flux_a = edge(ya, ya_in, jnp.where(even, has_up, has_down))
    flux_b = edge(yb, yb_in, jnp.where(even, has_down, has_up))
    top[...] = jnp.where(even, flux_a, flux_b)
    bottom[...] = jnp.where(even, flux_b, flux_a)
    kx = half_table(axial, None, axial.shape[0])
    inner = iota((GROUP, LANES), 1) == jnp.where(core == 0, LANES - 1, 0)
    row = iota((GROUP, LANES), 0)
    block = BLOCK
    blocks = ny // GROUP // block

    @pl.loop(0, blocks)
    def _(b):
        def rows(g):
            return pl.ds(pl.multiple_of((b * block + g) * GROUP, GROUP), GROUP)

        z_flux = []
        for g in range(block):
            own, other = z[rows(g)], z_in[rows(g)]
            z_flux.append(pltpu.roll(own + other, LANES - nx, 1) * (other - own))
        low = jnp.where(b == 0, 1.0, 0.0)
        high = jnp.where(b == blocks - 1, 1.0, 0.0)

        def source(i, g):
            s = s_ref[i, rows(g)]
            s = jnp.where(inner, s + jnp.broadcast_to(z_flux[g][:, i : i + 1], s.shape), s)
            if g == 0:
                s = jnp.where(row == 0, s + low * bottom[i : i + 1, :], s)
            if g == block - 1:
                s = jnp.where(row == GROUP - 1, s + high * top[i : i + 1, :], s)
            return s

        one = jnp.ones((GROUP, LANES), F32)
        state = []
        for g in range(block):
            first, here = pick(kx, kind_ref[0, rows(g)]), pick(kx, kind_ref[1, rows(g)])
            send_ref[b * block + g, 3] = first
            state.append((one, first + here, one, here, source(0, g), source(1, g)))
        for i in range(1, nx - 1):
            for g in range(block):
                first_ground, mutual, ground, here, first_value, value = state[g]
                after = pick(kx, kind_ref[i + 1, rows(g)])
                face = here + after
                r = reciprocal(ground + (mutual + face))
                t = face * r
                e = mutual * r
                t_ref[i, rows(g)] = t
                e_ref[i, rows(g)] = e
                q_ref[i, rows(g)] = value * r
                state[g] = (
                    first_ground + e * ground,
                    mutual * t,
                    1.0 + t * ground,
                    after,
                    first_value + e * value,
                    source(i + 1, g) + t * value,
                )
        for g in range(block):
            first_ground, mutual, ground, here, first_value, value = state[g]
            for n, item in zip((0, 1, 2, 4, 5, 6), (first_ground, mutual, ground, here, first_value, value)):
                send_ref[b * block + g, n] = item


def reduced_kernel(parts, got, out):
    half = parts // 2

    def inward(order, head):
        ends = (0, 2, 3, 4, 5, 6) if head else (2, 0, 4, 3, 6, 5)
        near, far, near_k, far_k, near_y, far_y = ends
        state = None
        steps = []
        for p in order:
            ground, value = got[p, near], got[p, near_y]
            joint = None
            if state is None:
                ground = ground + got[p, near_k]
            else:
                g, y, k = state
                face = k + got[p, near_k]
                r = reciprocal(g + face)
                t = face * r
                joint = (y * r, t)
                ground, value = ground + t * g, value + t * y
            m = got[p, 1]
            r = reciprocal(ground + m)
            t = m * r
            steps.append((p, joint, (value * r, t)))
            state = (got[p, far] + t * ground, got[p, far_y] + t * value, got[p, far_k])
        return state, steps

    left, left_steps = inward(range(half), True)
    right, right_steps = inward(range(parts - 1, half - 1, -1), False)
    face = left[2] + right[2]
    r = reciprocal(left[0] + face)
    t = face * r
    right_end = (right[1] + t * left[1]) * reciprocal(right[0] + t * left[0])
    left_end = left[1] * r + t * right_end

    def outward(steps, value, near, far):
        for p, joint, (base, slope) in reversed(steps):
            out[p, far] = value
            value = base + slope * value
            out[p, near] = value
            if joint is not None:
                value = joint[0] + joint[1] * value

    outward(left_steps, left_end, 0, 1)
    outward(right_steps, right_end, 1, 0)


def back_kernel(nx, ny, ends, q_ref, t_ref, e_ref, out_hbm, out, sems):
    block = 4
    count = ny // GROUP // block
    copies = []
    for b in range(count):

        def rows(g):
            return pl.ds((b * block + g) * GROUP, GROUP)

        head = [ends[b * block + g, 0] for g in range(block)]
        value = [ends[b * block + g, 1] for g in range(block)]
        for g in range(block):
            out[0, rows(g)] = head[g]
            out[nx - 1, rows(g)] = value[g]
        for i in range(nx - 2, 0, -1):
            for g in range(block):
                known = q_ref[i, rows(g)] + e_ref[i, rows(g)] * head[g]
                value[g] = known + t_ref[i, rows(g)] * value[g]
                out[i, rows(g)] = value[g]
        part = pl.ds(b * block * GROUP, block * GROUP)
        copy = pltpu.make_async_copy(out.at[:, part], out_hbm.at[:, part], sems.at[b])
        copy.start()
        copies.append(copy)
    for copy in copies:
        copy.wait()


def near(x):
    return pltpu.with_memory_space_constraint(x, pltpu.VMEM)


def far(x):
    return pltpu.with_memory_space_constraint(x, pltpu.HBM)


def call(kernel, name, outs, in_specs, out_specs, scratch=(), cost=(0, 0)):
    return pl.pallas_call(
        kernel,
        name=name,
        out_shape=outs,
        in_specs=in_specs,
        out_specs=out_specs,
        scratch_shapes=list(scratch),
        compiler_params=pltpu.CompilerParams(vmem_limit_bytes=VMEM_LIMIT),
        cost_estimate=pl.CostEstimate(flops=cost[0], bytes_accessed=cost[1], transcendentals=0),
    )


def per_device(u, kinds, axial, cross):
    nx, ny, nz = u.shape
    parts = lax.axis_size("gx")
    rows_of_y = lax.axis_size("gy")
    groups = ny // GROUP
    cells = nx * ny * nz
    field = pltpu.VMEM((nx, ny, nz), F32)
    y_face = pltpu.VMEM((2, nx, nz), F32)
    z_face = pltpu.VMEM((ny, LANES), F32)
    u_here, kind_here, ya, yb, z = call(
        functools.partial(faces_kernel, nx, ny),
        "faces",
        (field, pltpu.VMEM((nx, ny, nz), jnp.int32), y_face, y_face, z_face),
        [SMEM_SPEC, ANY_SPEC, ANY_SPEC],
        (VMEM_SPEC,) * 5,
        [pltpu.VMEM((ny, LANES), jnp.int32), pltpu.SemaphoreType.DMA((2, CHUNKS))],
        (2 * cells, 8 * cells),
    )(cross, far(u), far(kinds))
    odd_pairs = [(i, i ^ 1) for i in range(rows_of_y)]
    even_pairs = [(i, (i + 1 if i % 2 else i - 1) % rows_of_y) for i in range(rows_of_y)]
    ya_in = lax.ppermute(ya, "gy", odd_pairs)
    yb_in = lax.ppermute(yb, "gy", even_pairs)
    z_in = lax.ppermute(z, "gz", [(0, 1), (1, 0)])
    kind_here = near(kind_here)
    s = call(
        functools.partial(source_kernel, nx, ny),
        "source",
        field,
        [SMEM_SPEC, VMEM_SPEC, VMEM_SPEC],
        VMEM_SPEC,
        cost=(60 * cells, 8 * cells),
    )(cross, near(u_here), kind_here)
    t, e, q, send = call(
        functools.partial(sweep_kernel, nx, ny),
        "sweep",
        (field, field, field, pltpu.VMEM((groups, 7, GROUP, LANES), F32)),
        [SMEM_SPEC] + [VMEM_SPEC] * 8,
        (VMEM_SPEC,) * 4,
        [pltpu.VMEM((nx, nz), F32), pltpu.VMEM((nx, nz), F32)],
        (40 * cells, 8 * cells),
    )(axial, *map(near, (ya, yb, z, ya_in, yb_in, z_in, kind_here, s)))
    got = lax.all_to_all(send, "gx", 0, 0, tiled=True)
    solved = call(
        functools.partial(reduced_kernel, parts),
        "reduced",
        pltpu.VMEM((parts, 2, GROUP, LANES), F32),
        [VMEM_SPEC],
        VMEM_SPEC,
    )(near(got))
    ends = lax.all_to_all(solved, "gx", 0, 0, tiled=True)
    return call(
        functools.partial(back_kernel, nx, ny),
        "back",
        jax.ShapeDtypeStruct((nx, ny, nz), F32),
        [VMEM_SPEC] * 4,
        ANY_SPEC,
        [pltpu.VMEM((nx, ny, nz), F32), pltpu.SemaphoreType.DMA((ny // GROUP // 4,))],
        (4 * cells, 8 * cells),
    )(*map(near, (ends, q, t, e)))


def solution(mesh):
    placed = (P("gx", "gy", "gz"), P("gx", "gy", "gz"), P(), P())
    return jax.shard_map(
        per_device, mesh=mesh, in_specs=placed, out_specs=P("gx", "gy", "gz"), check_vma=False
    )
```

profile of v0, /device:TPU:0, one launch (start us, length us, event | category | flops | bytes accessed | tf_op | source)
XLA Modules:
  0.0 46.7 jit_solution(16029111721106973996)
XLA Ops:
  0.0 0.0 copy-start
  0.0 0.7 %copy-done = f32[2,8]{1,0:T(2,128)S(1)} copy-done((f32[2,8]{1,0:T(2,128)S(1)}, f32[2,8]{1,0:T(2,128)}, u32[]{:S(2)}) %copy-start) | copy-done | bytes 88
  0.7 3.9 %faces.1 = (f32[32,128,128]{2,1,0:T(8,128)S(1)}, s32[32,128,128]{2,1,0:T(8,128)S(1)}, f32[2,32,128]{2,1,0:T(8,128)S(1)}, f32[2,32,128]{2,1,0:T(8,128)S(1)}, f32[128,128]{1,0:T(8,128)S(1)}) custom-call(f32[2,8]{1,0:T(2,128)S(1)} %copy-done, f32[32,128,128]{2,1,0:T(8,128)} %u_hbm.1, s32[32,128,128]{2,1,0:T(8,128)} %kind_hbm.1), custom_call_target="tpu_custom_call" | custom-call | flops 1048576 | bytes 4194304 | tf_op jit(solution)/shard_map/faces/pallas_call | solution.py:312
  4.6 0.1 collective-permute-start.2
  4.7 2.1 %collective-permute-start = (f32[2,32,128]{2,1,0:T(8,128)S(1)}, f32[2,32,128]{2,1,0:T(8,128)S(1)}, u32[]{:S(2)}, u32[]{:S(2)}) collective-permute-start(f32[2,32,128]{2,1,0:T(8,128)S(1)} %get-tuple-element.14.ya), channel_id=1, source_target_pairs={{0,2},{2,0},{4,6},{6,4},{1,3},{3,1},{5,7},{7,5},{8,10},{10,8},{12,... | collective-permute-start | bytes 98312 | tf_op jit(solution)/shard_map/ppermute | solution.py:323
  6.8 2.5 %collective-permute-start.1 = (f32[2,32,128]{2,1,0:T(8,128)S(1)}, f32[2,32,128]{2,1,0:T(8,128)S(1)}, u32[]{:S(2)}, u32[]{:S(2)}) collective-permute-start(f32[2,32,128]{2,1,0:T(8,128)S(1)} %get-tuple-element.15.yb), channel_id=1, source_target_pairs={{0,6},{2,4},{4,2},{6,0},{1,7},{3,5},{5,3},{7,1},{8,14},{10,12},{12... | collective-permute-start | bytes 98312 | tf_op jit(solution)/shard_map/ppermute | solution.py:324
  9.3 0.0 copy-start.1
  9.3 3.8 %source.1.s_ref = f32[32,128,128]{2,1,0:T(8,128)S(1)} custom-call(f32[2,8]{1,0:T(2,128)S(1)} %copy-done, f32[32,128,128]{2,1,0:T(8,128)S(1)} %get-tuple-element.18.u_ref, s32[32,128,128]{2,1,0:T(8,128)S(1)} %get-tuple-element.17.kind_ref), custom_call_target="tpu_custom_call" | custom-call | flops 31457280 | bytes 4194304 | tf_op jit(solution)/shard_map/source/pallas_call | solution.py:327
  13.1 0.0 collective-permute-done.ya_in
  13.1 0.0 collective-permute-done.1.yb_in
  13.1 0.0 collective-permute-done.2.z_in
  13.1 0.0 copy-done.1
  13.1 3.1 %sweep.1 = (f32[32,128,128]{2,1,0:T(8,128)S(1)}, f32[32,128,128]{2,1,0:T(8,128)S(1)}, f32[32,128,128]{2,1,0:T(8,128)S(1)}, f32[16,7,8,128]{3,2,1,0:T(8,128)S(1)}) custom-call(f32[8]{0:T(128)S(1)} %copy-done.1, f32[2,32,128]{2,1,0:T(8,128)S(1)} %get-tuple-element.14.ya, f32[2,32,128]{2,1,0:T(8,128)S(1)} %get-tuple-element.15.yb, ...), custom_call_target="tpu_custom_call" | custom-call | flops 20971520 | bytes 4194304 | tf_op jit(solution)/shard_map/sweep/pallas_call | solution.py:335
  16.2 17.7 %all_to_all.10.got = f32[16,7,8,128]{3,2,1,0:T(8,128)S(1)} all-to-all(f32[16,7,8,128]{3,2,1,0:T(8,128)S(1)} %get-tuple-element.19), channel_id=1, replica_groups=mesh['gx'=16,'gy'=4,'gz'=2] {'gx'}, dimensions={0} | all-to-all | bytes 917504 | tf_op jit(solution)/shard_map/all_to_all | solution.py:344
  33.8 0.2 reduced.1
  34.1 11.1 %all_to_all.11.ends = f32[16,2,8,128]{3,2,1,0:T(8,128)S(1)} all-to-all(f32[16,2,8,128]{3,2,1,0:T(8,128)S(1)} %reduced.1), channel_id=1, replica_groups=mesh['gx'=16,'gy'=4,'gz'=2] {'gx'}, dimensions={0} | all-to-all | bytes 262144 | tf_op jit(solution)/shard_map/all_to_all | solution.py:352
  45.2 1.4 %back.1 = f32[32,128,128]{2,1,0:T(8,128)} custom-call(f32[16,2,8,128]{3,2,1,0:T(8,128)S(1)} %all_to_all.11.ends, f32[32,128,128]{2,1,0:T(8,128)S(1)} %get-tuple-element.20.q_ref, f32[32,128,128]{2,1,0:T(8,128)S(1)} %get-tuple-element.21.t_ref, f32[32,128,128]{2,1,0:T(8,128)S(1)} %get-tuple-element.22.e_ref), custom_call_target="tpu_custom_call" | custom-call | flops 2097152 | bytes 4194304 | tf_op jit(solution)/shard_map/back/pallas_call | solution.py:353
Async XLA Ops:
  0.0 0.7 %copy-start = (f32[2,8]{1,0:T(2,128)S(1)}, f32[2,8]{1,0:T(2,128)}, u32[]{:S(2)}) copy-start(f32[2,8]{1,0:T(2,128)} %cross.3) | copy-start | bytes 196
  4.6 8.5 %collective-permute-start.2 = (f32[128,128]{1,0:T(8,128)S(1)}, f32[128,128]{1,0:T(8,128)S(1)}, u32[]{:S(2)}, u32[]{:S(2)}) collective-permute-start(f32[128,128]{1,0:T(8,128)S(1)} %get-tuple-element.16.z), channel_id=1, source_target_pairs={{0,1},{1,0},{2,3},{3,2},{4,5},{5,4},{6,7},{7,6},{8,9},{9,8},{10,11... | collective-permute-start | bytes 196616 | tf_op jit(solution)/shard_map/ppermute | solution.py:325
  4.7 8.4 %collective-permute-start = (f32[2,32,128]{2,1,0:T(8,128)S(1)}, f32[2,32,128]{2,1,0:T(8,128)S(1)}, u32[]{:S(2)}, u32[]{:S(2)}) collective-permute-start(f32[2,32,128]{2,1,0:T(8,128)S(1)} %get-tuple-element.14.ya), channel_id=1, source_target_pairs={{0,2},{2,0},{4,6},{6,4},{1,3},{3,1},{5,7},{7,5},{8,10},{10,8},{12,... | collective-permute-start | bytes 98312 | tf_op jit(solution)/shard_map/ppermute | solution.py:323
  6.8 6.3 %collective-permute-start.1 = (f32[2,32,128]{2,1,0:T(8,128)S(1)}, f32[2,32,128]{2,1,0:T(8,128)S(1)}, u32[]{:S(2)}, u32[]{:S(2)}) collective-permute-start(f32[2,32,128]{2,1,0:T(8,128)S(1)} %get-tuple-element.15.yb), channel_id=1, source_target_pairs={{0,6},{2,4},{4,2},{6,0},{1,7},{3,5},{5,3},{7,1},{8,14},{10,12},{12... | collective-permute-start | bytes 98312 | tf_op jit(solution)/shard_map/ppermute | solution.py:324
  9.3 3.8 %copy-start.1 = (f32[8]{0:T(128)S(1)}, f32[8]{0:T(128)}, u32[]{:S(2)}) copy-start(f32[8]{0:T(128)} %axial.1) | copy-start | bytes 100
where the time goes:
time: 46.9 us; the launch traced here: 46.7 us
  blocking collectives  28.8 us (61%)
  Pallas kernels  12.4 us (26%)
  starting transfers between devices  4.69 us (10%)
  local copies, waits for them, and re-layouts  0.68 us (1%)
    all_to_all x1, blocking collectives, per_device(): got = lax.all_to_all(send, 'gx', 0, 0, tiled=True)  17.7 us
    all_to_all x1, blocking collectives, per_device(): ends = lax.all_to_all(solved, 'gx', 0, 0, tiled=True)  11.1 us
    pallas_call x1, Pallas kernels, per_device(): call(functools.partial(faces_kernel, nx, ny), 'faces', (field, pltpu.VMEM...  3.92 us
    pallas_call x1, Pallas kernels, per_device(): call(functools.partial(source_kernel, nx, ny), 'source', field, [SMEM_SPE...  3.76 us
    pallas_call x1, Pallas kernels, per_device(): call(functools.partial(sweep_kernel, nx, ny), 'sweep', (field, field, fie...  3.05 us
    ppermute x1, starting transfers between devices, per_device(): yb_in = lax.ppermute(yb, 'gy', even_pairs)  2.52 us
    ppermute x1, starting transfers between devices, per_device(): ya_in = lax.ppermute(ya, 'gy', odd_pairs)  2.08 us
    pallas_call x1, Pallas kernels, per_device(): call(functools.partial(back_kernel, nx, ny), 'back', jax.ShapeDtypeStruct...  1.44 us
  transfers between devices with their start and end apart: 3, of which 0 were waited for; matrix products, arithmetic and copies ran while one was open for 0% of the time, Pallas kernels for 8%

commit v1 on v0

v1 whole, which is shorter than its diff:
```python
import functools

import jax
import jax.numpy as jnp
from jax import lax
from jax.experimental import pallas as pl
from jax.experimental.pallas import tpu as pltpu
from jax.sharding import PartitionSpec as P

F32 = jnp.float32
LANES = 128
GROUP = 8
VMEM_LIMIT = 12 * 1024 * 1024
CHUNKS = 8
BLOCK = 16
SMEM_SPEC = pl.BlockSpec(memory_space=pltpu.SMEM)
VMEM_SPEC = pl.BlockSpec(memory_space=pltpu.VMEM)
ANY_SPEC = pl.BlockSpec(memory_space=pl.ANY)


def iota(shape, axis):
    return lax.broadcasted_iota(jnp.int32, shape, axis)


def half_table(table, row, classes):
    return [(table[c] if row is None else table[row, c]) * 0.5 for c in range(classes)]


def choose(table, bits):
    level = list(table)
    for bit in bits:
        half = len(level) // 2
        level = [jnp.where(bit, high, low) for low, high in zip(level[:half], level[half:])]
    return level[0]


def pick(tables, kinds):
    bits = kinds >= 4, (kinds & 2) != 0, (kinds & 1) != 0
    return [choose(table, bits) for table in tables]


def reciprocal(x):
    r = pl.reciprocal(x, approx=True)
    return r * (2.0 - x * r)


def local_kernel(
    nx, ny, axial_hbm, cross_hbm, u_hbm, kind_hbm, s_ref, x_ref, ya_ref, yb_ref, z_ref,
    u_ref, kind_ref, axial, cross, sems, table_sems,
):
    table_copies = [
        pltpu.make_async_copy(axial_hbm, axial, table_sems.at[0]),
        pltpu.make_async_copy(cross_hbm, cross, table_sems.at[1]),
    ]
    for copy in table_copies:
        copy.start()
    step = nx // CHUNKS
    copies = []
    for c in range(CHUNKS):
        part = pl.ds(c * step, step)
        pair = (
            pltpu.make_async_copy(kind_hbm.at[part], kind_ref.at[part], sems.at[1, c]),
            pltpu.make_async_copy(u_hbm.at[part], u_ref.at[part], sems.at[0, c]),
        )
        for copy in pair:
            copy.start()
        copies.append(pair)
    for copy in table_copies:
        copy.wait()
    classes = axial.shape[0]
    kx = half_table(axial, None, classes)
    ky = half_table(cross, 0, classes)
    kz = half_table(cross, 1, classes)
    even = lax.axis_index("gy") % 2 == 0
    core = lax.axis_index("gz")
    inner = jnp.where(core == 0, LANES - 1, 0)
    lane = iota((GROUP, LANES), 1)
    row = iota((GROUP, LANES), 0)
    outer = lane == LANES - 1 - inner
    groups = ny // GROUP

    def fetch(i, g):
        rows = pl.ds(g * GROUP, GROUP)
        u = u_ref[i, rows]
        hx, hy, hz = pick((kx, ky, kz), kind_ref[i, rows])
        x_ref[i, rows] = hx
        return u, hz, hy, pltpu.roll(u, GROUP - 1, 0), pltpu.roll(hy, GROUP - 1, 0)

    for i in range(nx):
        if i % step == 0:
            for copy in copies[i // step]:
                copy.wait()
        shift = lax.rem(LANES + i - inner, LANES)
        shift_k = lax.rem(LANES + nx + i - inner, LANES)
        now = fetch(i, 0)
        below = jnp.zeros((GROUP, LANES), F32)
        for g in range(groups):
            u, hz, hy, u_rolled, hy_rolled = now
            if g < groups - 1:
                now = fetch(i, g + 1)
                u_up = jnp.where(row == GROUP - 1, now[3], u_rolled)
                hy_up = jnp.where(row == GROUP - 1, now[4], hy_rolled)
                flux = (hy + hy_up) * (u_up - u)
            else:
                flux = jnp.where(row == GROUP - 1, 0.0, (hy + hy_rolled) * (u_rolled - u))
            down = pltpu.roll(flux, 1, 0)
            total = u + flux - jnp.where(row == 0, below, down)
            below = down
            z_up = (hz + pltpu.roll(hz, LANES - 1, 1)) * (pltpu.roll(u, LANES - 1, 1) - u)
            z_down = (hz + pltpu.roll(hz, 1, 1)) * (u - pltpu.roll(u, 1, 1))
            total = total + (jnp.where(lane == LANES - 1, 0.0, z_up) - jnp.where(lane == 0, 0.0, z_down))
            rows = pl.ds(g * GROUP, GROUP)
            s_ref[i, rows] = jnp.where(outer, total - hz * u, total)
            packed = z_ref[rows] if i else jnp.zeros((GROUP, LANES), F32)
            packed = jnp.where(lane == i, pltpu.roll(u, shift, 1), packed)
            z_ref[rows] = jnp.where(lane == nx + i, pltpu.roll(hz, shift_k, 1), packed)
    u_top, u_bottom = u_ref[:, ny - 1, :], u_ref[:, 0, :]
    k_top, k_bottom = pick((ky,), kind_ref[:, ny - 1, :])[0], pick((ky,), kind_ref[:, 0, :])[0]
    ya_ref[0] = jnp.where(even, u_top, u_bottom)
    ya_ref[1] = jnp.where(even, k_top, k_bottom)
    yb_ref[0] = jnp.where(even, u_bottom, u_top)
    yb_ref[1] = jnp.where(even, k_bottom, k_top)


def coefficients_kernel(nx, ny, x_ref, t_ref, e_ref, r_ref, net_ref):
    for b in range(ny // GROUP // BLOCK):

        def rows(g):
            return pl.ds((b * BLOCK + g) * GROUP, GROUP)

        one = jnp.ones((GROUP, LANES), F32)
        state = []
        for g in range(BLOCK):
            first, here = x_ref[0, rows(g)], x_ref[1, rows(g)]
            net_ref[b * BLOCK + g, 3] = first
            state.append((one, first + here, one, here))
        for i in range(1, nx - 1):
            for g in range(BLOCK):
                first_ground, mutual, ground, here = state[g]
                after = x_ref[i + 1, rows(g)]
                face = here + after
                r = reciprocal(ground + (mutual + face))
                t = face * r
                e = mutual * r
                t_ref[i, rows(g)] = t
                e_ref[i, rows(g)] = e
                r_ref[i, rows(g)] = r
                state[g] = (first_ground + e * ground, mutual * t, 1.0 + t * ground, after)
        for g in range(BLOCK):
            for n, item in zip((0, 1, 2, 4), state[g]):
                net_ref[b * BLOCK + g, n] = item


def forward_kernel(
    nx, ny, ya, yb, z, ya_in, yb_in, z_in, s_ref, t_ref, e_ref, r_ref, net_ref, q_ref, send_ref, top, bottom
):
    at, last = lax.axis_index("gy"), lax.axis_size("gy") - 1
    even = at % 2 == 0
    core = lax.axis_index("gz")

    def edge(own, other, inside):
        keep = jnp.where(inside, 1.0, 0.0)
        return (own[1] + other[1] * keep) * (other[0] * keep - own[0])

    has_up, has_down = at < last, at > 0
    flux_a = edge(ya, ya_in, jnp.where(even, has_up, has_down))
    flux_b = edge(yb, yb_in, jnp.where(even, has_down, has_up))
    top[...] = jnp.where(even, flux_a, flux_b)
    bottom[...] = jnp.where(even, flux_b, flux_a)
    inner = iota((GROUP, LANES), 1) == jnp.where(core == 0, LANES - 1, 0)
    row = iota((GROUP, LANES), 0)
    blocks = ny // GROUP // BLOCK
    for b in range(blocks):

        def rows(g):
            return pl.ds((b * BLOCK + g) * GROUP, GROUP)

        z_flux = []
        for g in range(BLOCK):
            own, other = z[rows(g)], z_in[rows(g)]
            z_flux.append(pltpu.roll(own + other, LANES - nx, 1) * (other - own))

        def source(i, g):
            s = s_ref[i, rows(g)]
            s = jnp.where(inner, s + jnp.broadcast_to(z_flux[g][:, i : i + 1], s.shape), s)
            if b == 0 and g == 0:
                s = jnp.where(row == 0, s + bottom[i : i + 1, :], s)
            if b == blocks - 1 and g == BLOCK - 1:
                s = jnp.where(row == GROUP - 1, s + top[i : i + 1, :], s)
            return s

        first = [source(0, g) for g in range(BLOCK)]
        value = [source(1, g) for g in range(BLOCK)]
        for i in range(1, nx - 1):
            for g in range(BLOCK):
                q_ref[i, rows(g)] = r_ref[i, rows(g)] * value[g]
                first[g] = first[g] + e_ref[i, rows(g)] * value[g]
                value[g] = source(i + 1, g) + t_ref[i, rows(g)] * value[g]
        for g in range(BLOCK):
            for n in range(5):
                send_ref[b * BLOCK + g, n] = net_ref[b * BLOCK + g, n]
            send_ref[b * BLOCK + g, 5] = first[g]
            send_ref[b * BLOCK + g, 6] = value[g]


def reduced_kernel(parts, got, out):
    half = parts // 2

    def inward(order, head):
        ends = (0, 2, 3, 4, 5, 6) if head else (2, 0, 4, 3, 6, 5)
        near, far, near_k, far_k, near_y, far_y = ends
        state = None
        steps = []
        for p in order:
            ground, value = got[p, near], got[p, near_y]
            joint = None
            if state is None:
                ground = ground + got[p, near_k]
            else:
                g, y, k = state
                face = k + got[p, near_k]
                r = reciprocal(g + face)
                t = face * r
                joint = (y * r, t)
                ground, value = ground + t * g, value + t * y
            m = got[p, 1]
            r = reciprocal(ground + m)
            t = m * r
            steps.append((p, joint, (value * r, t)))
            state = (got[p, far] + t * ground, got[p, far_y] + t * value, got[p, far_k])
        return state, steps

    left, left_steps = inward(range(half), True)
    right, right_steps = inward(range(parts - 1, half - 1, -1), False)
    face = left[2] + right[2]
    r = reciprocal(left[0] + face)
    t = face * r
    right_end = (right[1] + t * left[1]) * reciprocal(right[0] + t * left[0])
    left_end = left[1] * r + t * right_end

    def outward(steps, value, near, far):
        for p, joint, (base, slope) in reversed(steps):
            out[p, far] = value
            value = base + slope * value
            out[p, near] = value
            if joint is not None:
                value = joint[0] + joint[1] * value

    outward(left_steps, left_end, 0, 1)
    outward(right_steps, right_end, 1, 0)


def back_kernel(nx, ny, ends, q_ref, t_ref, e_ref, out_hbm, out, sems):
    block = 4
    count = ny // GROUP // block
    copies = []
    for b in range(count):

        def rows(g):
            return pl.ds((b * block + g) * GROUP, GROUP)

        head = [ends[b * block + g, 0] for g in range(block)]
        value = [ends[b * block + g, 1] for g in range(block)]
        for g in range(block):
            out[0, rows(g)] = head[g]
            out[nx - 1, rows(g)] = value[g]
        for i in range(nx - 2, 0, -1):
            for g in range(block):
                known = q_ref[i, rows(g)] + e_ref[i, rows(g)] * head[g]
                value[g] = known + t_ref[i, rows(g)] * value[g]
                out[i, rows(g)] = value[g]
        part = pl.ds(b * block * GROUP, block * GROUP)
        copy = pltpu.make_async_copy(out.at[:, part], out_hbm.at[:, part], sems.at[b])
        copy.start()
        copies.append(copy)
    for copy in copies:
        copy.wait()


def near(x):
    return pltpu.with_memory_space_constraint(x, pltpu.VMEM)


def far(x):
    return pltpu.with_memory_space_constraint(x, pltpu.HBM)


def call(kernel, name, outs, in_specs, out_specs, scratch=(), cost=(0, 0)):
    return pl.pallas_call(
        kernel,
        name=name,
        out_shape=outs,
        in_specs=in_specs,
        out_specs=out_specs,
        scratch_shapes=list(scratch),
        compiler_params=pltpu.CompilerParams(vmem_limit_bytes=VMEM_LIMIT),
        cost_estimate=pl.CostEstimate(flops=cost[0], bytes_accessed=cost[1], transcendentals=0),
    )


def per_device(u, kinds, axial, cross):
    nx, ny, nz = u.shape
    parts = lax.axis_size("gx")
    rows_of_y = lax.axis_size("gy")
    groups = ny // GROUP
    cells = nx * ny * nz
    field = pltpu.VMEM((nx, ny, nz), F32)
    y_face = pltpu.VMEM((2, nx, nz), F32)
    z_face = pltpu.VMEM((ny, LANES), F32)
    s, x, ya, yb, z = call(
        functools.partial(local_kernel, nx, ny),
        "local",
        (field, field, y_face, y_face, z_face),
        [ANY_SPEC] * 4,
        (VMEM_SPEC,) * 5,
        [
            pltpu.VMEM((nx, ny, nz), F32),
            pltpu.VMEM((nx, ny, nz), jnp.int32),
            pltpu.SMEM(axial.shape, F32),
            pltpu.SMEM(cross.shape, F32),
            pltpu.SemaphoreType.DMA((2, CHUNKS)),
            pltpu.SemaphoreType.DMA((2,)),
        ],
        (60 * cells, 8 * cells),
    )(*map(far, (axial, cross, u, kinds)))
    odd_pairs = [(i, i ^ 1) for i in range(rows_of_y)]
    even_pairs = [(i, (i + 1 if i % 2 else i - 1) % rows_of_y) for i in range(rows_of_y)]
    ya_in = lax.ppermute(ya, "gy", odd_pairs)
    yb_in = lax.ppermute(yb, "gy", even_pairs)
    z_in = lax.ppermute(z, "gz", [(0, 1), (1, 0)])
    t, e, r, net = call(
        functools.partial(coefficients_kernel, nx, ny),
        "coefficients",
        (field, field, field, pltpu.VMEM((groups, 5, GROUP, LANES), F32)),
        [VMEM_SPEC],
        (VMEM_SPEC,) * 4,
        cost=(80 * cells, 8 * cells),
    )(near(x))
    q, send = call(
        functools.partial(forward_kernel, nx, ny),
        "forward",
        (field, pltpu.VMEM((groups, 7, GROUP, LANES), F32)),
        [VMEM_SPEC] * 11,
        (VMEM_SPEC,) * 2,
        [pltpu.VMEM((nx, nz), F32), pltpu.VMEM((nx, nz), F32)],
        (10 * cells, 8 * cells),
    )(*map(near, (ya, yb, z, ya_in, yb_in, z_in, s, t, e, r, net)))
    got = lax.all_to_all(send, "gx", 0, 0, tiled=True)
    solved = call(
        functools.partial(reduced_kernel, parts),
        "reduced",
        pltpu.VMEM((parts, 2, GROUP, LANES), F32),
        [VMEM_SPEC],
        VMEM_SPEC,
    )(near(got))
    ends = lax.all_to_all(solved, "gx", 0, 0, tiled=True)
    return call(
        functools.partial(back_kernel, nx, ny),
        "back",
        jax.ShapeDtypeStruct((nx, ny, nz), F32),
        [VMEM_SPEC] * 4,
        ANY_SPEC,
        [pltpu.VMEM((nx, ny, nz), F32), pltpu.SemaphoreType.DMA((ny // GROUP // 4,))],
        (4 * cells, 8 * cells),
    )(*map(near, (ends, q, t, e)))


def solution(mesh):
    placed = (P("gx", "gy", "gz"), P("gx", "gy", "gz"), P(), P())
    return jax.shard_map(
        per_device, mesh=mesh, in_specs=placed, out_specs=P("gx", "gy", "gz"), check_vma=False
    )
```

time: 46.9 us -> 43.3 us (0.923)
  Pallas kernels: 12.4 us -> 9.05 us
  waiting for transfers between devices: 0.01 us -> 1.49 us
  blocking collectives: 28.8 us -> 27.9 us
  local copies, waits for them, and re-layouts: 0.68 us -> 0 us
    pallas_call x3, Pallas kernels: 10.7 us -> 7.39 us  [the longest x1 5.53 us: per_device(): call(functools.partial(local_kernel, nx, ny), 'local', (field, field, y_f...]
    ppermute x1, waiting for transfers between devices: 0.01 us -> 1.48 us  [per_device(): yb_in = lax.ppermute(yb, 'gy', even_pairs)]
    all_to_all x1, blocking collectives: 17.7 us -> 16.8 us  [per_device(): got = lax.all_to_all(send, 'gx', 0, 0, tiled=True)]
    unnamed x4 -> x0, local copies, waits for them, and re-layouts: 0.68 us -> none
  transfers between devices with their start and end apart: 3 -> 3, of which waited for: 0 -> 1; matrix products, arithmetic and copies ran while one was open for 0% -> 0% of each run, Pallas kernels for 8% -> 3%
where the time goes in v1:
time: 43.3 us; the launch traced here: 43.2 us
  blocking collectives  27.9 us (64%)
  Pallas kernels  9.05 us (21%)
  starting transfers between devices  4.69 us (11%)
  waiting for transfers between devices  1.49 us (3%)
    all_to_all x1, blocking collectives, per_device(): got = lax.all_to_all(send, 'gx', 0, 0, tiled=True)  16.8 us
    all_to_all x1, blocking collectives, per_device(): ends = lax.all_to_all(solved, 'gx', 0, 0, tiled=True)  11.1 us
    pallas_call x1, Pallas kernels, per_device(): call(functools.partial(local_kernel, nx, ny), 'local', (field, field, y_f...  5.53 us
    ppermute x1, starting transfers between devices, per_device(): yb_in = lax.ppermute(yb, 'gy', even_pairs)  2.52 us
    ppermute x1, starting transfers between devices, per_device(): ya_in = lax.ppermute(ya, 'gy', odd_pairs)  2.08 us
    ppermute x1, waiting for transfers between devices, per_device(): yb_in = lax.ppermute(yb, 'gy', even_pairs)  1.48 us
    pallas_call x1, Pallas kernels, per_device(): call(functools.partial(back_kernel, nx, ny), 'back', jax.ShapeDtypeStruct...  1.42 us
    pallas_call x1, Pallas kernels, per_device(): call(functools.partial(coefficients_kernel, nx, ny), 'coefficients', (fie...  1.1 us
  transfers between devices with their start and end apart: 3, of which 1 were waited for; matrix products, arithmetic and copies ran while one was open for 0% of the time, Pallas kernels for 3%

profile of v1, /device:TPU:0, one launch (start us, length us, event | category | flops | bytes accessed | tf_op | source)
XLA Modules:
  0.0 43.2 jit_solution(3704932412971301763)
XLA Ops:
  0.0 5.5 %local.1 = (f32[32,128,128]{2,1,0:T(8,128)S(1)}, f32[32,128,128]{2,1,0:T(8,128)S(1)}, f32[2,32,128]{2,1,0:T(8,128)S(1)}, f32[2,32,128]{2,1,0:T(8,128)S(1)}, f32[128,128]{1,0:T(8,128)S(1)}) custom-call(f32[8]{0:T(128)} %axial_hbm.1, f32[2,8]{1,0:T(2,128)} %cross_hbm.1, f32[32,128,128]{2,1,0:T(8,128)} %u_hbm.1, s32[32,128,128]{2,1,0:T(8,128)} %kind_hbm.1), custom_call_target="tpu_custom_call" | custom-call | flops 31457280 | bytes 4194304 | tf_op jit(solution)/shard_map/local/pallas_call | solution.py:310
  5.5 0.1 collective-permute-start.2
  5.6 2.1 %collective-permute-start = (f32[2,32,128]{2,1,0:T(8,128)S(1)}, f32[2,32,128]{2,1,0:T(8,128)S(1)}, u32[]{:S(2)}, u32[]{:S(2)}) collective-permute-start(f32[2,32,128]{2,1,0:T(8,128)S(1)} %get-tuple-element.16.ya), channel_id=1, source_target_pairs={{0,2},{2,0},{4,6},{6,4},{1,3},{3,1},{5,7},{7,5},{8,10},{10,8},{12,... | collective-permute-start | bytes 98312 | tf_op jit(solution)/shard_map/ppermute | solution.py:328
  7.7 2.5 %collective-permute-start.1 = (f32[2,32,128]{2,1,0:T(8,128)S(1)}, f32[2,32,128]{2,1,0:T(8,128)S(1)}, u32[]{:S(2)}, u32[]{:S(2)}) collective-permute-start(f32[2,32,128]{2,1,0:T(8,128)S(1)} %get-tuple-element.17.yb), channel_id=1, source_target_pairs={{0,6},{2,4},{4,2},{6,0},{1,7},{3,5},{5,3},{7,1},{8,14},{10,12},{12... | collective-permute-start | bytes 98312 | tf_op jit(solution)/shard_map/ppermute | solution.py:329
  10.2 1.1 %coefficients.1 = (f32[32,128,128]{2,1,0:T(8,128)S(1)}, f32[32,128,128]{2,1,0:T(8,128)S(1)}, f32[32,128,128]{2,1,0:T(8,128)S(1)}, f32[16,5,8,128]{3,2,1,0:T(8,128)S(1)}) custom-call(f32[32,128,128]{2,1,0:T(8,128)S(1)} %get-tuple-element.20.x_ref), custom_call_target="tpu_custom_call" | custom-call | flops 41943040 | bytes 4194304 | tf_op jit(solution)/shard_map/coefficients/pallas_call | solution.py:331
  11.3 0.0 collective-permute-done.ya_in
  11.3 1.5 %collective-permute-done.1.yb_in = f32[2,32,128]{2,1,0:T(8,128)S(1)} collective-permute-done((f32[2,32,128]{2,1,0:T(8,128)S(1)}, f32[2,32,128]{2,1,0:T(8,128)S(1)}, u32[]{:S(2)}, u32[]{:S(2)}) %collective-permute-start.1) | collective-permute-done | bytes 32800 | tf_op jit(solution)/shard_map/ppermute | solution.py:329
  12.8 0.0 collective-permute-done.2.z_in
  12.8 0.8 %forward.1 = (f32[32,128,128]{2,1,0:T(8,128)S(1)}, f32[16,7,8,128]{3,2,1,0:T(8,128)S(1)}) custom-call(f32[2,32,128]{2,1,0:T(8,128)S(1)} %get-tuple-element.16.ya, f32[2,32,128]{2,1,0:T(8,128)S(1)} %get-tuple-element.17.yb, f32[128,128]{1,0:T(8,128)S(1)} %get-tuple-element.18.z, f32[2,32,128]{2,1,0:T(8,128)S(1)} %collective-permute-done.ya_in, ...), custom_call_target="tpu_custom_call" | custom-call | flops 5242880 | bytes 4194304 | tf_op jit(solution)/shard_map/forward/pallas_call | solution.py:339
  13.6 16.8 %all_to_all.10.got = f32[16,7,8,128]{3,2,1,0:T(8,128)S(1)} all-to-all(f32[16,7,8,128]{3,2,1,0:T(8,128)S(1)} %get-tuple-element.25), channel_id=1, replica_groups=mesh['gx'=16,'gy'=4,'gz'=2] {'gx'}, dimensions={0} | all-to-all | bytes 917504 | tf_op jit(solution)/shard_map/all_to_all | solution.py:348
  30.4 0.2 reduced.1
  30.6 11.1 %all_to_all.11.ends = f32[16,2,8,128]{3,2,1,0:T(8,128)S(1)} all-to-all(f32[16,2,8,128]{3,2,1,0:T(8,128)S(1)} %reduced.1), channel_id=1, replica_groups=mesh['gx'=16,'gy'=4,'gz'=2] {'gx'}, dimensions={0} | all-to-all | bytes 262144 | tf_op jit(solution)/shard_map/all_to_all | solution.py:356
  41.7 1.4 %back.1 = f32[32,128,128]{2,1,0:T(8,128)} custom-call(f32[16,2,8,128]{3,2,1,0:T(8,128)S(1)} %all_to_all.11.ends, f32[32,128,128]{2,1,0:T(8,128)S(1)} %get-tuple-element.26.q_ref, f32[32,128,128]{2,1,0:T(8,128)S(1)} %get-tuple-element.21.t_ref, f32[32,128,128]{2,1,0:T(8,128)S(1)} %get-tuple-element.22.e_ref), custom_call_target="tpu_custom_call" | custom-call | flops 2097152 | bytes 4194304 | tf_op jit(solution)/shard_map/back/pallas_call | solution.py:357
Async XLA Ops:
  5.5 7.3 %collective-permute-start.2 = (f32[128,128]{1,0:T(8,128)S(1)}, f32[128,128]{1,0:T(8,128)S(1)}, u32[]{:S(2)}, u32[]{:S(2)}) collective-permute-start(f32[128,128]{1,0:T(8,128)S(1)} %get-tuple-element.18.z), channel_id=1, source_target_pairs={{0,1},{1,0},{2,3},{3,2},{4,5},{5,4},{6,7},{7,6},{8,9},{9,8},{10,11... | collective-permute-start | bytes 196616 | tf_op jit(solution)/shard_map/ppermute | solution.py:330
  5.6 5.7 %collective-permute-start = (f32[2,32,128]{2,1,0:T(8,128)S(1)}, f32[2,32,128]{2,1,0:T(8,128)S(1)}, u32[]{:S(2)}, u32[]{:S(2)}) collective-permute-start(f32[2,32,128]{2,1,0:T(8,128)S(1)} %get-tuple-element.16.ya), channel_id=1, source_target_pairs={{0,2},{2,0},{4,6},{6,4},{1,3},{3,1},{5,7},{7,5},{8,10},{10,8},{12,... | collective-permute-start | bytes 98312 | tf_op jit(solution)/shard_map/ppermute | solution.py:328
  7.7 5.1 %collective-permute-start.1 = (f32[2,32,128]{2,1,0:T(8,128)S(1)}, f32[2,32,128]{2,1,0:T(8,128)S(1)}, u32[]{:S(2)}, u32[]{:S(2)}) collective-permute-start(f32[2,32,128]{2,1,0:T(8,128)S(1)} %get-tuple-element.17.yb), channel_id=1, source_target_pairs={{0,6},{2,4},{4,2},{6,0},{1,7},{3,5},{5,3},{7,1},{8,14},{10,12},{12... | collective-permute-start | bytes 98312 | tf_op jit(solution)/shard_map/ppermute | solution.py:329

commit v2 on v1

--- a/solution.py
+++ b/solution.py
@@ -45,8 +45,9 @@
 
 
 def local_kernel(
-    nx, ny, axial_hbm, cross_hbm, u_hbm, kind_hbm, s_ref, x_ref, ya_ref, yb_ref, z_ref,
-    u_ref, kind_ref, axial, cross, sems, table_sems,
+    nx, ny, axial_hbm, cross_hbm, u_hbm, kind_hbm,
+    u_ref, hy_ref, hz_ref, t_ref, e_ref, r_ref, net_ref, ya_ref, yb_ref, z_ref,
+    kind_ref, axial, cross, sems, table_sems,
 ):
     table_copies = [
         pltpu.make_async_copy(axial_hbm, axial, table_sems.at[0]),
@@ -72,34 +73,71 @@
     ky = half_table(cross, 0, classes)
     kz = half_table(cross, 1, classes)
     even = lax.axis_index("gy") % 2 == 0
-    core = lax.axis_index("gz")
-    inner = jnp.where(core == 0, LANES - 1, 0)
+    inner = jnp.where(lax.axis_index("gz") == 0, LANES - 1, 0)
     lane = iota((GROUP, LANES), 1)
-    row = iota((GROUP, LANES), 0)
-    outer = lane == LANES - 1 - inner
     groups = ny // GROUP
-
-    def fetch(i, g):
-        rows = pl.ds(g * GROUP, GROUP)
-        u = u_ref[i, rows]
-        hx, hy, hz = pick((kx, ky, kz), kind_ref[i, rows])
-        x_ref[i, rows] = hx
-        return u, hz, hy, pltpu.roll(u, GROUP - 1, 0), pltpu.roll(hy, GROUP - 1, 0)
-
+    one = jnp.ones((GROUP, LANES), F32)
+    state = [None] * groups
     for i in range(nx):
         if i % step == 0:
             for copy in copies[i // step]:
                 copy.wait()
         shift = lax.rem(LANES + i - inner, LANES)
         shift_k = lax.rem(LANES + nx + i - inner, LANES)
+        for g in range(groups):
+            rows = pl.ds(g * GROUP, GROUP)
+            after, hy, hz = pick((kx, ky, kz), kind_ref[i, rows])
+            hy_ref[i, rows] = hy
+            hz_ref[i, rows] = hz
+            packed = z_ref[rows] if i else jnp.zeros((GROUP, LANES), F32)
+            packed = jnp.where(lane == i, pltpu.roll(u_ref[i, rows], shift, 1), packed)
+            z_ref[rows] = jnp.where(lane == nx + i, pltpu.roll(hz, shift_k, 1), packed)
+            if i == 0:
+                net_ref[g, 3] = after
+                state[g] = after
+            elif i == 1:
+                state[g] = (one, state[g] + after, one, after)
+            else:
+                first_ground, mutual, ground, here = state[g]
+                face = here + after
+                r = reciprocal(ground + (mutual + face))
+                t = face * r
+                e = mutual * r
+                t_ref[i - 1, rows] = t
+                e_ref[i - 1, rows] = e
+                r_ref[i - 1, rows] = r
+                state[g] = (first_ground + e * ground, mutual * t, 1.0 + t * ground, after)
+    for g in range(groups):
+        for n, item in zip((0, 1, 2, 4), state[g]):
+            net_ref[g, n] = item
+    ya_ref[0] = jnp.where(even, u_ref[:, ny - 1, :], u_ref[:, 0, :])
+    ya_ref[1] = jnp.where(even, hy_ref[:, ny - 1, :], hy_ref[:, 0, :])
+    yb_ref[0] = jnp.where(even, u_ref[:, 0, :], u_ref[:, ny - 1, :])
+    yb_ref[1] = jnp.where(even, hy_ref[:, 0, :], hy_ref[:, ny - 1, :])
+
+
+def source_kernel(nx, ny, u_ref, hy_ref, hz_ref, s_ref):
+    lane = iota((GROUP, LANES), 1)
+    row = iota((GROUP, LANES), 0)
+    outer = lane == jnp.where(lax.axis_index("gz") == 0, 0, LANES - 1)
+    groups = ny // GROUP
+
+    def fetch(i, g):
+        rows = pl.ds(g * GROUP, GROUP)
+        u, hy = u_ref[i, rows], hy_ref[i, rows]
+        return u, hy, pltpu.roll(u, GROUP - 1, 0), pltpu.roll(hy, GROUP - 1, 0)
+
+    for i in range(nx):
         now = fetch(i, 0)
         below = jnp.zeros((GROUP, LANES), F32)
         for g in range(groups):
-            u, hz, hy, u_rolled, hy_rolled = now
+            rows = pl.ds(g * GROUP, GROUP)
+            u, hy, u_rolled, hy_rolled = now
+            hz = hz_ref[i, rows]
             if g < groups - 1:
                 now = fetch(i, g + 1)
-                u_up = jnp.where(row == GROUP - 1, now[3], u_rolled)
-                hy_up = jnp.where(row == GROUP - 1, now[4], hy_rolled)
+                u_up = jnp.where(row == GROUP - 1, now[2], u_rolled)
+                hy_up = jnp.where(row == GROUP - 1, now[3], hy_rolled)
                 flux = (hy + hy_up) * (u_up - u)
             else:
                 flux = jnp.where(row == GROUP - 1, 0.0, (hy + hy_rolled) * (u_rolled - u))
@@ -109,46 +147,7 @@
             z_up = (hz + pltpu.roll(hz, LANES - 1, 1)) * (pltpu.roll(u, LANES - 1, 1) - u)
             z_down = (hz + pltpu.roll(hz, 1, 1)) * (u - pltpu.roll(u, 1, 1))
             total = total + (jnp.where(lane == LANES - 1, 0.0, z_up) - jnp.where(lane == 0, 0.0, z_down))
-            rows = pl.ds(g * GROUP, GROUP)
             s_ref[i, rows] = jnp.where(outer, total - hz * u, total)
-            packed = z_ref[rows] if i else jnp.zeros((GROUP, LANES), F32)
-            packed = jnp.where(lane == i, pltpu.roll(u, shift, 1), packed)
-            z_ref[rows] = jnp.where(lane == nx + i, pltpu.roll(hz, shift_k, 1), packed)
-    u_top, u_bottom = u_ref[:, ny - 1, :], u_ref[:, 0, :]
-    k_top, k_bottom = pick((ky,), kind_ref[:, ny - 1, :])[0], pick((ky,), kind_ref[:, 0, :])[0]
-    ya_ref[0] = jnp.where(even, u_top, u_bottom)
-    ya_ref[1] = jnp.where(even, k_top, k_bottom)
-    yb_ref[0] = jnp.where(even, u_bottom, u_top)
-    yb_ref[1] = jnp.where(even, k_bottom, k_top)
-
-
-def coefficients_kernel(nx, ny, x_ref, t_ref, e_ref, r_ref, net_ref):
-    for b in range(ny // GROUP // BLOCK):
-
-        def rows(g):
-            return pl.ds((b * BLOCK + g) * GROUP, GROUP)
-
-        one = jnp.ones((GROUP, LANES), F32)
-        state = []
-        for g in range(BLOCK):
-            first, here = x_ref[0, rows(g)], x_ref[1, rows(g)]
-            net_ref[b * BLOCK + g, 3] = first
-            state.append((one, first + here, one, here))
-        for i in range(1, nx - 1):
-            for g in range(BLOCK):
-                first_ground, mutual, ground, here = state[g]
-                after = x_ref[i + 1, rows(g)]
-                face = here + after
-                r = reciprocal(ground + (mutual + face))
-                t = face * r
-                e = mutual * r
-                t_ref[i, rows(g)] = t
-                e_ref[i, rows(g)] = e
-                r_ref[i, rows(g)] = r
-                state[g] = (first_ground + e * ground, mutual * t, 1.0 + t * ground, after)
-        for g in range(BLOCK):
-            for n, item in zip((0, 1, 2, 4), state[g]):
-                net_ref[b * BLOCK + g, n] = item
 
 
 def forward_kernel(
@@ -307,14 +306,13 @@
     field = pltpu.VMEM((nx, ny, nz), F32)
     y_face = pltpu.VMEM((2, nx, nz), F32)
     z_face = pltpu.VMEM((ny, LANES), F32)
-    s, x, ya, yb, z = call(
+    u_here, hy, hz, t, e, r, net, ya, yb, z = call(
         functools.partial(local_kernel, nx, ny),
         "local",
-        (field, field, y_face, y_face, z_face),
+        (field,) * 6 + (pltpu.VMEM((groups, 5, GROUP, LANES), F32), y_face, y_face, z_face),
         [ANY_SPEC] * 4,
-        (VMEM_SPEC,) * 5,
+        (VMEM_SPEC,) * 10,
         [
-            pltpu.VMEM((nx, ny, nz), F32),
             pltpu.VMEM((nx, ny, nz), jnp.int32),
             pltpu.SMEM(axial.shape, F32),
             pltpu.SMEM(cross.shape, F32),
@@ -324,18 +322,23 @@
         (60 * cells, 8 * cells),
     )(*map(far, (axial, cross, u, kinds)))
     odd_pairs = [(i, i ^ 1) for i in range(rows_of_y)]
-    even_pairs = [(i, (i + 1 if i % 2 else i - 1) % rows_of_y) for i in range(rows_of_y)]
+    even_pairs = [
+        (2 * i + c, 2 * j + c if 0 <= j < rows_of_y else 2 * i + 1 - c)
+        for i in range(rows_of_y)
+        for j in (i + 1 if i % 2 else i - 1,)
+        for c in range(2)
+    ]
     ya_in = lax.ppermute(ya, "gy", odd_pairs)
-    yb_in = lax.ppermute(yb, "gy", even_pairs)
+    yb_in = lax.ppermute(yb, ("gy", "gz"), even_pairs)
     z_in = lax.ppermute(z, "gz", [(0, 1), (1, 0)])
-    t, e, r, net = call(
-        functools.partial(coefficients_kernel, nx, ny),
-        "coefficients",
-        (field, field, field, pltpu.VMEM((groups, 5, GROUP, LANES), F32)),
-        [VMEM_SPEC],
-        (VMEM_SPEC,) * 4,
+    s = call(
+        functools.partial(source_kernel, nx, ny),
+        "source",
+        field,
+        [VMEM_SPEC] * 3,
+        VMEM_SPEC,
         cost=(80 * cells, 8 * cells),
-    )(near(x))
+    )(*map(near, (u_here, hy, hz)))
     q, send = call(
         functools.partial(forward_kernel, nx, ny),
         "forward",

time: 43.3 us -> 42 us (0.970)
  the two profiles are of different devices: /device:TPU:0 before, /device:TPU:32 now
where the time goes in v2:
time: 42 us; the launch traced here: 41.9 us
  blocking collectives  28.8 us (69%)
  Pallas kernels  9.31 us (22%)
  starting transfers between devices  3.71 us (9%)
    all_to_all x1, blocking collectives, per_device(): got = lax.all_to_all(send, 'gx', 0, 0, tiled=True)  17.7 us
    all_to_all x1, blocking collectives, per_device(): ends = lax.all_to_all(solved, 'gx', 0, 0, tiled=True)  11.1 us
    pallas_call x1, Pallas kernels, per_device(): call(functools.partial(local_kernel, nx, ny), 'local', (field,) * 6 + (pl...  4.65 us
    ppermute x1, starting transfers between devices, per_device(): yb_in = lax.ppermute(yb, ('gy', 'gz'), even_pairs)  3.52 us
    pallas_call x1, Pallas kernels, per_device(): call(functools.partial(source_kernel, nx, ny), 'source', field, [VMEM_SPE...  2.22 us
    pallas_call x1, Pallas kernels, per_device(): call(functools.partial(back_kernel, nx, ny), 'back', jax.ShapeDtypeStruct...  1.42 us
  transfers between devices with their start and end apart: 3, of which 0 were waited for; matrix products, arithmetic and copies ran while one was open for 0% of the time, Pallas kernels for 5%

profile of v2, /device:TPU:32, one launch (start us, length us, event | category | flops | bytes accessed | tf_op | source)
XLA Modules:
  0.0 41.9 jit_solution(14444320310050174897)
XLA Ops:
  0.0 4.7 %local.1 = (f32[32,128,128]{2,1,0:T(8,128)S(1)}, f32[32,128,128]{2,1,0:T(8,128)S(1)}, f32[32,128,128]{2,1,0:T(8,128)S(1)}, f32[32,128,128]{2,1,0:T(8,128)S(1)}, ...) custom-call(f32[8]{0:T(128)} %axial_hbm.1, ...), custom_call_target="tpu_custom_call" | custom-call | flops 31457280 | bytes 4194304 | tf_op jit(solution)/shard_map/local/pallas_call | solution.py:309
  4.7 0.1 collective-permute-start.2
  4.8 0.1 collective-permute-start
  4.9 3.5 %collective-permute-start.1 = (f32[2,32,128]{2,1,0:T(8,128)S(1)}, f32[2,32,128]{2,1,0:T(8,128)S(1)}, u32[]{:S(2)}, u32[]{:S(2)}) collective-permute-start(f32[2,32,128]{2,1,0:T(8,128)S(1)} %get-tuple-element.18.yb), channel_id=1, source_target_pairs={{0,1},{1,0},{2,4},{3,5},{4,2},{5,3},{6,7},{7,6},{8,9},{9,8},{10,12... | collective-permute-start | bytes 98312 | tf_op jit(solution)/shard_map/ppermute | solution.py:332
  8.4 2.2 %source.1.s_ref = f32[32,128,128]{2,1,0:T(8,128)S(1)} custom-call(f32[32,128,128]{2,1,0:T(8,128)S(1)} %get-tuple-element.20.u_ref, f32[32,128,128]{2,1,0:T(8,128)S(1)} %get-tuple-element.21.hy_ref, f32[32,128,128]{2,1,0:T(8,128)S(1)} %get-tuple-element.22.hz_ref), custom_call_target="tpu_custom_call" | custom-call | flops 41943040 | bytes 4194304 | tf_op jit(solution)/shard_map/source/pallas_call | solution.py:334
  10.6 0.0 collective-permute-done.ya_in
  10.6 0.0 collective-permute-done.1.yb_in
  10.6 0.0 collective-permute-done.2.z_in
  10.6 0.8 %forward.1 = (f32[32,128,128]{2,1,0:T(8,128)S(1)}, f32[16,7,8,128]{3,2,1,0:T(8,128)S(1)}) custom-call(f32[2,32,128]{2,1,0:T(8,128)S(1)} %get-tuple-element.17.ya, f32[2,32,128]{2,1,0:T(8,128)S(1)} %get-tuple-element.18.yb, f32[128,128]{1,0:T(8,128)S(1)} %get-tuple-element.19.z, f32[2,32,128]{2,1,0:T(8,128)S(1)} %collective-permute-done.ya_in, ...), custom_call_target="tpu_custom_call" | custom-call | flops 5242880 | bytes 4194304 | tf_op jit(solution)/shard_map/forward/pallas_call | solution.py:342
  11.4 17.7 %all_to_all.10.got = f32[16,7,8,128]{3,2,1,0:T(8,128)S(1)} all-to-all(f32[16,7,8,128]{3,2,1,0:T(8,128)S(1)} %get-tuple-element.27), channel_id=1, replica_groups=mesh['gx'=16,'gy'=4,'gz'=2] {'gx'}, dimensions={0} | all-to-all | bytes 917504 | tf_op jit(solution)/shard_map/all_to_all | solution.py:351
  29.1 0.2 reduced.1
  29.3 11.1 %all_to_all.11.ends = f32[16,2,8,128]{3,2,1,0:T(8,128)S(1)} all-to-all(f32[16,2,8,128]{3,2,1,0:T(8,128)S(1)} %reduced.1), channel_id=1, replica_groups=mesh['gx'=16,'gy'=4,'gz'=2] {'gx'}, dimensions={0} | all-to-all | bytes 262144 | tf_op jit(solution)/shard_map/all_to_all | solution.py:359
  40.5 1.4 %back.1 = f32[32,128,128]{2,1,0:T(8,128)} custom-call(f32[16,2,8,128]{3,2,1,0:T(8,128)S(1)} %all_to_all.11.ends, f32[32,128,128]{2,1,0:T(8,128)S(1)} %get-tuple-element.28.q_ref, f32[32,128,128]{2,1,0:T(8,128)S(1)} %get-tuple-element.23.t_ref, f32[32,128,128]{2,1,0:T(8,128)S(1)} %get-tuple-element.24.e_ref), custom_call_target="tpu_custom_call" | custom-call | flops 2097152 | bytes 4194304 | tf_op jit(solution)/shard_map/back/pallas_call | solution.py:360
Async XLA Ops:
  4.7 6.0 %collective-permute-start.2 = (f32[128,128]{1,0:T(8,128)S(1)}, f32[128,128]{1,0:T(8,128)S(1)}, u32[]{:S(2)}, u32[]{:S(2)}) collective-permute-start(f32[128,128]{1,0:T(8,128)S(1)} %get-tuple-element.19.z), channel_id=1, source_target_pairs={{0,1},{1,0},{2,3},{3,2},{4,5},{5,4},{6,7},{7,6},{8,9},{9,8},{10,11... | collective-permute-start | bytes 196616 | tf_op jit(solution)/shard_map/ppermute | solution.py:333
  4.8 5.9 %collective-permute-start = (f32[2,32,128]{2,1,0:T(8,128)S(1)}, f32[2,32,128]{2,1,0:T(8,128)S(1)}, u32[]{:S(2)}, u32[]{:S(2)}) collective-permute-start(f32[2,32,128]{2,1,0:T(8,128)S(1)} %get-tuple-element.17.ya), channel_id=1, source_target_pairs={{0,2},{2,0},{4,6},{6,4},{1,3},{3,1},{5,7},{7,5},{8,10},{10,8},{12,... | collective-permute-start | bytes 98312 | tf_op jit(solution)/shard_map/ppermute | solution.py:331
  4.9 5.8 %collective-permute-start.1 = (f32[2,32,128]{2,1,0:T(8,128)S(1)}, f32[2,32,128]{2,1,0:T(8,128)S(1)}, u32[]{:S(2)}, u32[]{:S(2)}) collective-permute-start(f32[2,32,128]{2,1,0:T(8,128)S(1)} %get-tuple-element.18.yb), channel_id=1, source_target_pairs={{0,1},{1,0},{2,4},{3,5},{4,2},{5,3},{6,7},{7,6},{8,9},{9,8},{10,12... | collective-permute-start | bytes 98312 | tf_op jit(solution)/shard_map/ppermute | solution.py:332

commit v3 on v2

--- a/solution.py
+++ b/solution.py
@@ -11,7 +11,7 @@
 LANES = 128
 GROUP = 8
 VMEM_LIMIT = 12 * 1024 * 1024
-CHUNKS = 8
+CHUNKS = 4
 BLOCK = 16
 SMEM_SPEC = pl.BlockSpec(memory_space=pltpu.SMEM)
 VMEM_SPEC = pl.BlockSpec(memory_space=pltpu.VMEM)
@@ -46,7 +46,7 @@
 
 def local_kernel(
     nx, ny, axial_hbm, cross_hbm, u_hbm, kind_hbm,
-    u_ref, hy_ref, hz_ref, t_ref, e_ref, r_ref, net_ref, ya_ref, yb_ref, z_ref,
+    u_ref, x_ref, hy_ref, hz_ref, last_ref, ya_ref, yb_ref, z_ref,
     kind_ref, axial, cross, sems, table_sems,
 ):
     table_copies = [
@@ -76,8 +76,6 @@
     inner = jnp.where(lax.axis_index("gz") == 0, LANES - 1, 0)
     lane = iota((GROUP, LANES), 1)
     groups = ny // GROUP
-    one = jnp.ones((GROUP, LANES), F32)
-    state = [None] * groups
     for i in range(nx):
         if i % step == 0:
             for copy in copies[i // step]:
@@ -86,37 +84,24 @@
         shift_k = lax.rem(LANES + nx + i - inner, LANES)
         for g in range(groups):
             rows = pl.ds(g * GROUP, GROUP)
-            after, hy, hz = pick((kx, ky, kz), kind_ref[i, rows])
+            hx, hy, hz = pick((kx, ky, kz), kind_ref[i, rows])
+            x_ref[i, rows] = hx
+            if i == nx - 1:
+                last_ref[rows] = hx
             hy_ref[i, rows] = hy
             hz_ref[i, rows] = hz
             packed = z_ref[rows] if i else jnp.zeros((GROUP, LANES), F32)
             packed = jnp.where(lane == i, pltpu.roll(u_ref[i, rows], shift, 1), packed)
             z_ref[rows] = jnp.where(lane == nx + i, pltpu.roll(hz, shift_k, 1), packed)
-            if i == 0:
-                net_ref[g, 3] = after
-                state[g] = after
-            elif i == 1:
-                state[g] = (one, state[g] + after, one, after)
-            else:
-                first_ground, mutual, ground, here = state[g]
-                face = here + after
-                r = reciprocal(ground + (mutual + face))
-                t = face * r
-                e = mutual * r
-                t_ref[i - 1, rows] = t
-                e_ref[i - 1, rows] = e
-                r_ref[i - 1, rows] = r
-                state[g] = (first_ground + e * ground, mutual * t, 1.0 + t * ground, after)
-    for g in range(groups):
-        for n, item in zip((0, 1, 2, 4), state[g]):
-            net_ref[g, n] = item
     ya_ref[0] = jnp.where(even, u_ref[:, ny - 1, :], u_ref[:, 0, :])
     ya_ref[1] = jnp.where(even, hy_ref[:, ny - 1, :], hy_ref[:, 0, :])
     yb_ref[0] = jnp.where(even, u_ref[:, 0, :], u_ref[:, ny - 1, :])
     yb_ref[1] = jnp.where(even, hy_ref[:, 0, :], hy_ref[:, ny - 1, :])
 
 
-def source_kernel(nx, ny, u_ref, hy_ref, hz_ref, s_ref):
+def source_kernel(nx, ny, u_ref, x_ref, hy_ref, hz_ref, s_ref, t_ref, e_ref, r_ref, net_ref):
+    one = jnp.ones((GROUP, LANES), F32)
+    state = [None] * (ny // GROUP)
     lane = iota((GROUP, LANES), 1)
     row = iota((GROUP, LANES), 0)
     outer = lane == jnp.where(lax.axis_index("gz") == 0, 0, LANES - 1)
@@ -148,10 +133,30 @@
             z_down = (hz + pltpu.roll(hz, 1, 1)) * (u - pltpu.roll(u, 1, 1))
             total = total + (jnp.where(lane == LANES - 1, 0.0, z_up) - jnp.where(lane == 0, 0.0, z_down))
             s_ref[i, rows] = jnp.where(outer, total - hz * u, total)
+            after = x_ref[i, rows]
+            if i == 0:
+                net_ref[g, 3] = after
+                state[g] = after
+            elif i == 1:
+                state[g] = (one, state[g] + after, one, after)
+            else:
+                first_ground, mutual, ground, here = state[g]
+                face = here + after
+                r = reciprocal(ground + (mutual + face))
+                t = face * r
+                e = mutual * r
+                t_ref[i - 1, rows] = t
+                e_ref[i - 1, rows] = e
+                r_ref[i - 1, rows] = r
+                state[g] = (first_ground + e * ground, mutual * t, 1.0 + t * ground, after)
+    for g in range(groups):
+        for n, item in zip((0, 1, 2, 4), state[g]):
+            net_ref[g, n] = item
 
 
 def forward_kernel(
-    nx, ny, ya, yb, z, ya_in, yb_in, z_in, s_ref, t_ref, e_ref, r_ref, net_ref, q_ref, send_ref, top, bottom
+    nx, ny, left, ya, yb, z, ya_in, yb_in, z_in, s_ref, t_ref, e_ref, r_ref, net_ref,
+    q_ref, first_ref, send_ref, top, bottom,
 ):
     at, last = lax.axis_index("gy"), lax.axis_size("gy") - 1
     even = at % 2 == 0
@@ -166,6 +171,8 @@
     flux_b = edge(yb, yb_in, jnp.where(even, has_down, has_up))
     top[...] = jnp.where(even, flux_a, flux_b)
     bottom[...] = jnp.where(even, flux_b, flux_a)
+    part, parts = lax.axis_index("gx"), lax.axis_size("gx")
+    starts, ends = part == 0, part == parts - 1
     inner = iota((GROUP, LANES), 1) == jnp.where(core == 0, LANES - 1, 0)
     row = iota((GROUP, LANES), 0)
     blocks = ny // GROUP // BLOCK
@@ -196,60 +203,67 @@
                 first[g] = first[g] + e_ref[i, rows(g)] * value[g]
                 value[g] = source(i + 1, g) + t_ref[i, rows(g)] * value[g]
         for g in range(BLOCK):
-            for n in range(5):
-                send_ref[b * BLOCK + g, n] = net_ref[b * BLOCK + g, n]
-            send_ref[b * BLOCK + g, 5] = first[g]
-            send_ref[b * BLOCK + g, 6] = value[g]
+            at_group = b * BLOCK + g
+            first_ground, mutual, ground, first_half, last_half = (net_ref[at_group, n] for n in range(5))
+            before = left[rows(g)]
+            face = first_half + jnp.where(starts, 0.0, before)
+            r = reciprocal(first_ground + (mutual + face))
+            t = face * r
+            e = mutual * r
+            first_ref[at_group, 0] = r * first[g]
+            first_ref[at_group, 1] = t
+            first_ref[at_group, 2] = e
+            joint = mutual * t
+            ground = ground + e * first_ground
+            ground = jnp.where(starts, ground + joint, ground)
+            ground = jnp.where(ends, ground + last_half, ground)
+            send_ref[at_group, 0] = t * first_ground
+            send_ref[at_group, 1] = joint
+            send_ref[at_group, 2] = ground
+            send_ref[at_group, 3] = t * first[g]
+            send_ref[at_group, 4] = value[g] + e * first[g]
 
 
 def reduced_kernel(parts, got, out):
     half = parts // 2
-
-    def inward(order, head):
-        ends = (0, 2, 3, 4, 5, 6) if head else (2, 0, 4, 3, 6, 5)
-        near, far, near_k, far_k, near_y, far_y = ends
-        state = None
-        steps = []
-        for p in order:
-            ground, value = got[p, near], got[p, near_y]
-            joint = None
-            if state is None:
-                ground = ground + got[p, near_k]
-            else:
-                g, y, k = state
-                face = k + got[p, near_k]
-                r = reciprocal(g + face)
-                t = face * r
-                joint = (y * r, t)
-                ground, value = ground + t * g, value + t * y
-            m = got[p, 1]
-            r = reciprocal(ground + m)
-            t = m * r
-            steps.append((p, joint, (value * r, t)))
-            state = (got[p, far] + t * ground, got[p, far_y] + t * value, got[p, far_k])
-        return state, steps
-
-    left, left_steps = inward(range(half), True)
-    right, right_steps = inward(range(parts - 1, half - 1, -1), False)
-    face = left[2] + right[2]
-    r = reciprocal(left[0] + face)
-    t = face * r
-    right_end = (right[1] + t * left[1]) * reciprocal(right[0] + t * left[0])
-    left_end = left[1] * r + t * right_end
-
-    def outward(steps, value, near, far):
-        for p, joint, (base, slope) in reversed(steps):
-            out[p, far] = value
-            value = base + slope * value
-            out[p, near] = value
-            if joint is not None:
-                value = joint[0] + joint[1] * value
-
-    outward(left_steps, left_end, 0, 1)
-    outward(right_steps, right_end, 1, 0)
-
-
-def back_kernel(nx, ny, ends, q_ref, t_ref, e_ref, out_hbm, out, sems):
+    ground, value = got[0, 2], got[0, 4]
+    left = []
+    for p in range(1, half):
+        ground, value = ground + got[p, 0], value + got[p, 3]
+        m = got[p, 1]
+        r = reciprocal(ground + m)
+        t = m * r
+        left.append((value * r, t))
+        ground, value = got[p, 2] + t * ground, got[p, 4] + t * value
+    right = []
+    ground_r, value_r = got[parts - 1, 2], got[parts - 1, 4]
+    for p in range(parts - 1, half - 1, -1):
+        m = got[p, 1]
+        r = reciprocal(ground_r + m)
+        t = m * r
+        right.append((value_r * r, t))
+        ground_r, value_r = got[p, 0] + t * ground_r, got[p, 3] + t * value_r
+        if p > half:
+            ground_r, value_r = ground_r + got[p - 1, 2], value_r + got[p - 1, 4]
+    middle = (value + value_r) * reciprocal(ground + ground_r)
+    cell = middle
+    for p in range(half - 1, -1, -1):
+        out[p, 1] = cell
+        if p:
+            base, slope = left[p - 1]
+            cell = base + slope * cell
+            out[p, 0] = cell
+        else:
+            out[p, 0] = jnp.zeros_like(cell)
+    cell = middle
+    for p in range(half, parts):
+        base, slope = right[parts - 1 - p]
+        out[p, 0] = cell
+        cell = base + slope * cell
+        out[p, 1] = cell
+
+
+def back_kernel(nx, ny, ends, first, q_ref, t_ref, e_ref, out_hbm, out, sems):
     block = 4
     count = ny // GROUP // block
     copies = []
@@ -258,8 +272,11 @@
         def rows(g):
             return pl.ds((b * block + g) * GROUP, GROUP)
 
-        head = [ends[b * block + g, 0] for g in range(block)]
         value = [ends[b * block + g, 1] for g in range(block)]
+        head = []
+        for g in range(block):
+            at = b * block + g
+            head.append(first[at, 0] + first[at, 1] * ends[at, 0] + first[at, 2] * value[g])
         for g in range(block):
             out[0, rows(g)] = head[g]
             out[nx - 1, rows(g)] = value[g]
@@ -306,12 +323,12 @@
     field = pltpu.VMEM((nx, ny, nz), F32)
     y_face = pltpu.VMEM((2, nx, nz), F32)
     z_face = pltpu.VMEM((ny, LANES), F32)
-    u_here, hy, hz, t, e, r, net, ya, yb, z = call(
+    u_here, x, hy, hz, x_last, ya, yb, z = call(
         functools.partial(local_kernel, nx, ny),
         "local",
-        (field,) * 6 + (pltpu.VMEM((groups, 5, GROUP, LANES), F32), y_face, y_face, z_face),
+        (field,) * 4 + (z_face, y_face, y_face, z_face),
         [ANY_SPEC] * 4,
-        (VMEM_SPEC,) * 10,
+        (VMEM_SPEC,) * 8,
         [
             pltpu.VMEM((nx, ny, nz), jnp.int32),
             pltpu.SMEM(axial.shape, F32),
@@ -321,6 +338,7 @@
         ],
         (60 * cells, 8 * cells),
     )(*map(far, (axial, cross, u, kinds)))
+    left = lax.ppermute(x_last, "gx", [(i, (i + 1) % parts) for i in range(parts)])
     odd_pairs = [(i, i ^ 1) for i in range(rows_of_y)]
     even_pairs = [
         (2 * i + c, 2 * j + c if 0 <= j < rows_of_y else 2 * i + 1 - c)
@@ -331,23 +349,23 @@
     ya_in = lax.ppermute(ya, "gy", odd_pairs)
     yb_in = lax.ppermute(yb, ("gy", "gz"), even_pairs)
     z_in = lax.ppermute(z, "gz", [(0, 1), (1, 0)])
-    s = call(
+    s, t, e, r, net = call(
         functools.partial(source_kernel, nx, ny),
         "source",
-        field,
-        [VMEM_SPEC] * 3,
-        VMEM_SPEC,
+        (field,) * 4 + (pltpu.VMEM((groups, 5, GROUP, LANES), F32),),
+        [VMEM_SPEC] * 4,
+        (VMEM_SPEC,) * 5,
         cost=(80 * cells, 8 * cells),
-    )(*map(near, (u_here, hy, hz)))
-    q, send = call(
+    )(*map(near, (u_here, x, hy, hz)))
+    q, first, send = call(
         functools.partial(forward_kernel, nx, ny),
         "forward",
-        (field, pltpu.VMEM((groups, 7, GROUP, LANES), F32)),
-        [VMEM_SPEC] * 11,
-        (VMEM_SPEC,) * 2,
+        (field, pltpu.VMEM((groups, 3, GROUP, LANES), F32), pltpu.VMEM((groups, 5, GROUP, LANES), F32)),
+        [VMEM_SPEC] * 12,
+        (VMEM_SPEC,) * 3,
         [pltpu.VMEM((nx, nz), F32), pltpu.VMEM((nx, nz), F32)],
         (10 * cells, 8 * cells),
-    )(*map(near, (ya, yb, z, ya_in, yb_in, z_in, s, t, e, r, net)))
+    )(*map(near, (left, ya, yb, z, ya_in, yb_in, z_in, s, t, e, r, net)))
     got = lax.all_to_all(send, "gx", 0, 0, tiled=True)
     solved = call(
         functools.partial(reduced_kernel, parts),
@@ -361,11 +379,11 @@
         functools.partial(back_kernel, nx, ny),
         "back",
         jax.ShapeDtypeStruct((nx, ny, nz), F32),
-        [VMEM_SPEC] * 4,
+        [VMEM_SPEC] * 5,
         ANY_SPEC,
         [pltpu.VMEM((nx, ny, nz), F32), pltpu.SemaphoreType.DMA((ny // GROUP // 4,))],
         (4 * cells, 8 * cells),
-    )(*map(near, (ends, q, t, e)))
+    )(*map(near, (ends, first, q, t, e)))
 
 
 def solution(mesh):

time: 42 us -> 41.4 us (0.986)
  blocking collectives: 28.8 us -> 26.8 us
  starting transfers between devices: 3.71 us -> 5.27 us
    all_to_all x1, blocking collectives: 17.7 us -> 15.5 us  [per_device(): got = lax.all_to_all(send, 'gx', 0, 0, tiled=True)]
    ppermute x0 -> x1, starting transfers between devices: none -> 1.65 us  [per_device(): lax.ppermute(x_last, 'gx', [(i, (i + 1) % parts) for i in range(parts)])]
  transfers between devices with their start and end apart: 3 -> 4, of which waited for: 0 -> 0; matrix products, arithmetic and copies ran while one was open for 0% -> 0% of each run, Pallas kernels for 5% -> 8%
where the time goes in v3:
time: 41.4 us; the launch traced here: 41.2 us
  blocking collectives  26.8 us (65%)
  Pallas kernels  9.09 us (22%)
  starting transfers between devices  5.27 us (13%)
    all_to_all x1, blocking collectives, per_device(): got = lax.all_to_all(send, 'gx', 0, 0, tiled=True)  15.5 us
    all_to_all x1, blocking collectives, per_device(): ends = lax.all_to_all(solved, 'gx', 0, 0, tiled=True)  11.3 us
    pallas_call x1, Pallas kernels, per_device(): call(functools.partial(local_kernel, nx, ny), 'local', (field,) * 4 + (z_...  3.49 us
    ppermute x1, starting transfers between devices, per_device(): yb_in = lax.ppermute(yb, ('gy', 'gz'), even_pairs)  3.43 us
    pallas_call x1, Pallas kernels, per_device(): call(functools.partial(source_kernel, nx, ny), 'source', (field,) * 4 + (...  3.25 us
    ppermute x1, starting transfers between devices, per_device(): lax.ppermute(x_last, 'gx', [(i, (i + 1) % parts) for i in range(parts)])  1.65 us
    pallas_call x1, Pallas kernels, per_device(): call(functools.partial(back_kernel, nx, ny), 'back', jax.ShapeDtypeStruct...  1.42 us
  transfers between devices with their start and end apart: 4, of which 0 were waited for; matrix products, arithmetic and copies ran while one was open for 0% of the time, Pallas kernels for 8%

profile of v3, /device:TPU:32, one launch (start us, length us, event | category | flops | bytes accessed | tf_op | source)
XLA Modules:
  0.0 41.2 jit_solution(5607159795864434697)
XLA Ops:
  0.0 3.5 %local.1 = (f32[32,128,128]{2,1,0:T(8,128)S(1)}, f32[32,128,128]{2,1,0:T(8,128)S(1)}, f32[32,128,128]{2,1,0:T(8,128)S(1)}, f32[32,128,128]{2,1,0:T(8,128)S(1)}, ...) custom-call(f32[8]{0:T(128)} %axial_hbm.1, ...), custom_call_target="tpu_custom_call" | custom-call | flops 31457280 | bytes 4194304 | tf_op jit(solution)/shard_map/local/pallas_call | solution.py:326
  3.5 0.1 collective-permute-start.3
  3.6 1.6 %collective-permute-start = (f32[128,128]{1,0:T(8,128)S(1)}, f32[128,128]{1,0:T(8,128)S(1)}, u32[]{:S(2)}, u32[]{:S(2)}) collective-permute-start(f32[128,128]{1,0:T(8,128)S(1)} %get-tuple-element.21), channel_id=1, source_target_pairs={{0,8},{8,16},{16,24},{24,32},{32,40},{40,48},{48,56},{56,64},{64,7... | collective-permute-start | bytes 196616 | tf_op jit(solution)/shard_map/ppermute | solution.py:341
  5.2 0.1 collective-permute-start.1
  5.3 3.4 %collective-permute-start.2 = (f32[2,32,128]{2,1,0:T(8,128)S(1)}, f32[2,32,128]{2,1,0:T(8,128)S(1)}, u32[]{:S(2)}, u32[]{:S(2)}) collective-permute-start(f32[2,32,128]{2,1,0:T(8,128)S(1)} %get-tuple-element.23.yb), channel_id=1, source_target_pairs={{0,1},{1,0},{2,4},{3,5},{4,2},{5,3},{6,7},{7,6},{8,9},{9,8},{10,12... | collective-permute-start | bytes 98312 | tf_op jit(solution)/shard_map/ppermute | solution.py:350
  8.8 3.3 %source.1 = (f32[32,128,128]{2,1,0:T(8,128)S(1)}, f32[32,128,128]{2,1,0:T(8,128)S(1)}, f32[32,128,128]{2,1,0:T(8,128)S(1)}, f32[32,128,128]{2,1,0:T(8,128)S(1)}, f32[16,5,8,128]{3,2,1,0:T(8,128)S(1)}) custom-call(f32[32,128,128]{2,1,0:T(8,128)S(1)} %get-tuple-element.25.u_ref, f32[32,128,128]{2,1,0:T(8,128)S(1)} %get-tuple-element.26.x_ref, ...), custom_call_target="tpu_custom_call" | custom-call | flops 41943040 | bytes 4194304 | tf_op jit(solution)/shard_map/source/pallas_call | solution.py:352
  12.0 0.0 collective-permute-done.1.ya_in
  12.1 0.0 collective-permute-done.2.yb_in
  12.1 0.0 collective-permute-done.3.z_in
  12.1 0.0 collective-permute-done.left
  12.1 0.8 %forward.1 = (f32[32,128,128]{2,1,0:T(8,128)S(1)}, f32[16,3,8,128]{3,2,1,0:T(8,128)S(1)}, f32[16,5,8,128]{3,2,1,0:T(8,128)S(1)}) custom-call(f32[128,128]{1,0:T(8,128)S(1)} %collective-permute-done.left, f32[2,32,128]{2,1,0:T(8,128)S(1)} %get-tuple-element.22.ya, f32[2,32,128]{2,1,0:T(8,128)S(1)} %get-tuple-element.23.yb, ...), custom_call_target="tpu_custom_call" | custom-call | flops 5242880 | bytes 4194304 | tf_op jit(solution)/shard_map/forward/pallas_call | solution.py:360
  12.9 15.5 %all_to_all.10.got = f32[16,5,8,128]{3,2,1,0:T(8,128)S(1)} all-to-all(f32[16,5,8,128]{3,2,1,0:T(8,128)S(1)} %get-tuple-element.34), channel_id=1, replica_groups=mesh['gx'=16,'gy'=4,'gz'=2] {'gx'}, dimensions={0} | all-to-all | bytes 655360 | tf_op jit(solution)/shard_map/all_to_all | solution.py:369
  28.4 0.1 reduced.1
  28.5 11.3 %all_to_all.11.ends = f32[16,2,8,128]{3,2,1,0:T(8,128)S(1)} all-to-all(f32[16,2,8,128]{3,2,1,0:T(8,128)S(1)} %reduced.1), channel_id=1, replica_groups=mesh['gx'=16,'gy'=4,'gz'=2] {'gx'}, dimensions={0} | all-to-all | bytes 262144 | tf_op jit(solution)/shard_map/all_to_all | solution.py:377
  39.8 1.4 %back.1 = f32[32,128,128]{2,1,0:T(8,128)} custom-call(f32[16,2,8,128]{3,2,1,0:T(8,128)S(1)} %all_to_all.11.ends, f32[16,3,8,128]{3,2,1,0:T(8,128)S(1)} %get-tuple-element.35.first, f32[32,128,128]{2,1,0:T(8,128)S(1)} %get-tuple-element.36.q_ref, f32[32,128,128]{2,1,0:T(8,128)S(1)} %get-tuple-element.30.t_ref, f32[32,128,128]{2,1,0:T(8,128)S(1)} %get-tuple-element.31.e_ref), custom_call_target="tpu_custom_call" | custom-call | flops 2097152 | bytes 4194304 | tf_op jit(solution)/shard_map/back/pallas_call | solution.py:378
Async XLA Ops:
  3.5 8.6 %collective-permute-start.3 = (f32[128,128]{1,0:T(8,128)S(1)}, f32[128,128]{1,0:T(8,128)S(1)}, u32[]{:S(2)}, u32[]{:S(2)}) collective-permute-start(f32[128,128]{1,0:T(8,128)S(1)} %get-tuple-element.24.z), channel_id=1, source_target_pairs={{0,1},{1,0},{2,3},{3,2},{4,5},{5,4},{6,7},{7,6},{8,9},{9,8},{10,11... | collective-permute-start | bytes 196616 | tf_op jit(solution)/shard_map/ppermute | solution.py:351
  3.6 8.5 %collective-permute-start = (f32[128,128]{1,0:T(8,128)S(1)}, f32[128,128]{1,0:T(8,128)S(1)}, u32[]{:S(2)}, u32[]{:S(2)}) collective-permute-start(f32[128,128]{1,0:T(8,128)S(1)} %get-tuple-element.21), channel_id=1, source_target_pairs={{0,8},{8,16},{16,24},{24,32},{32,40},{40,48},{48,56},{56,64},{64,7... | collective-permute-start | bytes 196616 | tf_op jit(solution)/shard_map/ppermute | solution.py:341
  5.2 6.8 %collective-permute-start.1 = (f32[2,32,128]{2,1,0:T(8,128)S(1)}, f32[2,32,128]{2,1,0:T(8,128)S(1)}, u32[]{:S(2)}, u32[]{:S(2)}) collective-permute-start(f32[2,32,128]{2,1,0:T(8,128)S(1)} %get-tuple-element.22.ya), channel_id=1, source_target_pairs={{0,2},{2,0},{4,6},{6,4},{1,3},{3,1},{5,7},{7,5},{8,10},{10,8},{12,... | collective-permute-start | bytes 98312 | tf_op jit(solution)/shard_map/ppermute | solution.py:349
  5.3 6.7 %collective-permute-start.2 = (f32[2,32,128]{2,1,0:T(8,128)S(1)}, f32[2,32,128]{2,1,0:T(8,128)S(1)}, u32[]{:S(2)}, u32[]{:S(2)}) collective-permute-start(f32[2,32,128]{2,1,0:T(8,128)S(1)} %get-tuple-element.23.yb), channel_id=1, source_target_pairs={{0,1},{1,0},{2,4},{3,5},{4,2},{5,3},{6,7},{7,6},{8,9},{9,8},{10,12... | collective-permute-start | bytes 98312 | tf_op jit(solution)/shard_map/ppermute | solution.py:350

commit v4 on v2

--- a/solution.py
+++ b/solution.py
@@ -11,7 +11,7 @@
 LANES = 128
 GROUP = 8
 VMEM_LIMIT = 12 * 1024 * 1024
-CHUNKS = 8
+CHUNKS = 4
 BLOCK = 16
 SMEM_SPEC = pl.BlockSpec(memory_space=pltpu.SMEM)
 VMEM_SPEC = pl.BlockSpec(memory_space=pltpu.VMEM)
@@ -46,7 +46,7 @@
 
 def local_kernel(
     nx, ny, axial_hbm, cross_hbm, u_hbm, kind_hbm,
-    u_ref, hy_ref, hz_ref, t_ref, e_ref, r_ref, net_ref, ya_ref, yb_ref, z_ref,
+    u_ref, x_ref, hy_ref, hz_ref, ya_ref, yb_ref, z_ref,
     kind_ref, axial, cross, sems, table_sems,
 ):
     table_copies = [
@@ -76,8 +76,6 @@
     inner = jnp.where(lax.axis_index("gz") == 0, LANES - 1, 0)
     lane = iota((GROUP, LANES), 1)
     groups = ny // GROUP
-    one = jnp.ones((GROUP, LANES), F32)
-    state = [None] * groups
     for i in range(nx):
         if i % step == 0:
             for copy in copies[i // step]:
@@ -86,37 +84,22 @@
         shift_k = lax.rem(LANES + nx + i - inner, LANES)
         for g in range(groups):
             rows = pl.ds(g * GROUP, GROUP)
-            after, hy, hz = pick((kx, ky, kz), kind_ref[i, rows])
+            hx, hy, hz = pick((kx, ky, kz), kind_ref[i, rows])
+            x_ref[i, rows] = hx
             hy_ref[i, rows] = hy
             hz_ref[i, rows] = hz
             packed = z_ref[rows] if i else jnp.zeros((GROUP, LANES), F32)
             packed = jnp.where(lane == i, pltpu.roll(u_ref[i, rows], shift, 1), packed)
             z_ref[rows] = jnp.where(lane == nx + i, pltpu.roll(hz, shift_k, 1), packed)
-            if i == 0:
-                net_ref[g, 3] = after
-                state[g] = after
-            elif i == 1:
-                state[g] = (one, state[g] + after, one, after)
-            else:
-                first_ground, mutual, ground, here = state[g]
-                face = here + after
-                r = reciprocal(ground + (mutual + face))
-                t = face * r
-                e = mutual * r
-                t_ref[i - 1, rows] = t
-                e_ref[i - 1, rows] = e
-                r_ref[i - 1, rows] = r
-                state[g] = (first_ground + e * ground, mutual * t, 1.0 + t * ground, after)
-    for g in range(groups):
-        for n, item in zip((0, 1, 2, 4), state[g]):
-            net_ref[g, n] = item
     ya_ref[0] = jnp.where(even, u_ref[:, ny - 1, :], u_ref[:, 0, :])
     ya_ref[1] = jnp.where(even, hy_ref[:, ny - 1, :], hy_ref[:, 0, :])
     yb_ref[0] = jnp.where(even, u_ref[:, 0, :], u_ref[:, ny - 1, :])
     yb_ref[1] = jnp.where(even, hy_ref[:, 0, :], hy_ref[:, ny - 1, :])
 
 
-def source_kernel(nx, ny, u_ref, hy_ref, hz_ref, s_ref):
+def source_kernel(nx, ny, u_ref, x_ref, hy_ref, hz_ref, s_ref, t_ref, e_ref, r_ref, net_ref):
+    one = jnp.ones((GROUP, LANES), F32)
+    state = [None] * (ny // GROUP)
     lane = iota((GROUP, LANES), 1)
     row = iota((GROUP, LANES), 0)
     outer = lane == jnp.where(lax.axis_index("gz") == 0, 0, LANES - 1)
@@ -148,6 +131,25 @@
             z_down = (hz + pltpu.roll(hz, 1, 1)) * (u - pltpu.roll(u, 1, 1))
             total = total + (jnp.where(lane == LANES - 1, 0.0, z_up) - jnp.where(lane == 0, 0.0, z_down))
             s_ref[i, rows] = jnp.where(outer, total - hz * u, total)
+            after = x_ref[i, rows]
+            if i == 0:
+                net_ref[g, 3] = after
+                state[g] = after
+            elif i == 1:
+                state[g] = (one, state[g] + after, one, after)
+            else:
+                first_ground, mutual, ground, here = state[g]
+                face = here + after
+                r = reciprocal(ground + (mutual + face))
+                t = face * r
+                e = mutual * r
+                t_ref[i - 1, rows] = t
+                e_ref[i - 1, rows] = e
+                r_ref[i - 1, rows] = r
+                state[g] = (first_ground + e * ground, mutual * t, 1.0 + t * ground, after)
+    for g in range(groups):
+        for n, item in zip((0, 1, 2, 4), state[g]):
+            net_ref[g, n] = item
 
 
 def forward_kernel(
@@ -306,12 +308,12 @@
     field = pltpu.VMEM((nx, ny, nz), F32)
     y_face = pltpu.VMEM((2, nx, nz), F32)
     z_face = pltpu.VMEM((ny, LANES), F32)
-    u_here, hy, hz, t, e, r, net, ya, yb, z = call(
+    u_here, x, hy, hz, ya, yb, z = call(
         functools.partial(local_kernel, nx, ny),
         "local",
-        (field,) * 6 + (pltpu.VMEM((groups, 5, GROUP, LANES), F32), y_face, y_face, z_face),
+        (field,) * 4 + (y_face, y_face, z_face),
         [ANY_SPEC] * 4,
-        (VMEM_SPEC,) * 10,
+        (VMEM_SPEC,) * 7,
         [
             pltpu.VMEM((nx, ny, nz), jnp.int32),
             pltpu.SMEM(axial.shape, F32),
@@ -331,14 +333,14 @@
     ya_in = lax.ppermute(ya, "gy", odd_pairs)
     yb_in = lax.ppermute(yb, ("gy", "gz"), even_pairs)
     z_in = lax.ppermute(z, "gz", [(0, 1), (1, 0)])
-    s = call(
+    s, t, e, r, net = call(
         functools.partial(source_kernel, nx, ny),
         "source",
-        field,
-        [VMEM_SPEC] * 3,
-        VMEM_SPEC,
+        (field,) * 4 + (pltpu.VMEM((groups, 5, GROUP, LANES), F32),),
+        [VMEM_SPEC] * 4,
+        (VMEM_SPEC,) * 5,
         cost=(80 * cells, 8 * cells),
-    )(*map(near, (u_here, hy, hz)))
+    )(*map(near, (u_here, x, hy, hz)))
     q, send = call(
         functools.partial(forward_kernel, nx, ny),
         "forward",

time: 42 us -> 41.9 us (level)
  transfers between devices with their start and end apart: 3 -> 3, of which waited for: 0 -> 0; matrix products, arithmetic and copies ran while one was open for 0% -> 0% of each run, Pallas kernels for 5% -> 8%
where the time goes in v4:
time: 41.9 us; the launch traced here: 41.7 us
  blocking collectives  28.8 us (69%)
  Pallas kernels  9.17 us (22%)
  starting transfers between devices  3.71 us (9%)
    all_to_all x1, blocking collectives, per_device(): got = lax.all_to_all(send, 'gx', 0, 0, tiled=True)  17.7 us
    all_to_all x1, blocking collectives, per_device(): ends = lax.all_to_all(solved, 'gx', 0, 0, tiled=True)  11.1 us
    ppermute x1, starting transfers between devices, per_device(): yb_in = lax.ppermute(yb, ('gy', 'gz'), even_pairs)  3.52 us
    pallas_call x1, Pallas kernels, per_device(): call(functools.partial(local_kernel, nx, ny), 'local', (field,) * 4 + (y_...  3.49 us
    pallas_call x1, Pallas kernels, per_device(): call(functools.partial(source_kernel, nx, ny), 'source', (field,) * 4 + (...  3.25 us
    pallas_call x1, Pallas kernels, per_device(): call(functools.partial(back_kernel, nx, ny), 'back', jax.ShapeDtypeStruct...  1.42 us
  transfers between devices with their start and end apart: 3, of which 0 were waited for; matrix products, arithmetic and copies ran while one was open for 0% of the time, Pallas kernels for 8%

profile of v4, /device:TPU:32, one launch (start us, length us, event | category | flops | bytes accessed | tf_op | source)
XLA Modules:
  0.0 41.7 jit_solution(1469381760088870983)
XLA Ops:
  0.0 3.5 %local.1 = (f32[32,128,128]{2,1,0:T(8,128)S(1)}, f32[32,128,128]{2,1,0:T(8,128)S(1)}, f32[32,128,128]{2,1,0:T(8,128)S(1)}, f32[32,128,128]{2,1,0:T(8,128)S(1)}, ...) custom-call(f32[8]{0:T(128)} %axial_hbm.1, f32[2,8]{1,0:T(2,128)} %cross_hbm.1, ...), custom_call_target="tpu_custom_call" | custom-call | flops 31457280 | bytes 4194304 | tf_op jit(solution)/shard_map/local/pallas_call | solution.py:311
  3.5 0.1 collective-permute-start.2
  3.6 0.1 collective-permute-start
  3.7 3.5 %collective-permute-start.1 = (f32[2,32,128]{2,1,0:T(8,128)S(1)}, f32[2,32,128]{2,1,0:T(8,128)S(1)}, u32[]{:S(2)}, u32[]{:S(2)}) collective-permute-start(f32[2,32,128]{2,1,0:T(8,128)S(1)} %get-tuple-element.20.yb), channel_id=1, source_target_pairs={{0,1},{1,0},{2,4},{3,5},{4,2},{5,3},{6,7},{7,6},{8,9},{9,8},{10,12... | collective-permute-start | bytes 98312 | tf_op jit(solution)/shard_map/ppermute | solution.py:334
  7.2 3.3 %source.1 = (f32[32,128,128]{2,1,0:T(8,128)S(1)}, f32[32,128,128]{2,1,0:T(8,128)S(1)}, f32[32,128,128]{2,1,0:T(8,128)S(1)}, f32[32,128,128]{2,1,0:T(8,128)S(1)}, f32[16,5,8,128]{3,2,1,0:T(8,128)S(1)}) custom-call(f32[32,128,128]{2,1,0:T(8,128)S(1)} %get-tuple-element.22.u_ref, f32[32,128,128]{2,1,0:T(8,128)S(1)} %get-tuple-element.23.x_ref, ...), custom_call_target="tpu_custom_call" | custom-call | flops 41943040 | bytes 4194304 | tf_op jit(solution)/shard_map/source/pallas_call | solution.py:336
  10.5 0.0 collective-permute-done.ya_in
  10.5 0.0 collective-permute-done.1.yb_in
  10.5 0.0 collective-permute-done.2.z_in
  10.5 0.8 %forward.1 = (f32[32,128,128]{2,1,0:T(8,128)S(1)}, f32[16,7,8,128]{3,2,1,0:T(8,128)S(1)}) custom-call(f32[2,32,128]{2,1,0:T(8,128)S(1)} %get-tuple-element.19.ya, f32[2,32,128]{2,1,0:T(8,128)S(1)} %get-tuple-element.20.yb, f32[128,128]{1,0:T(8,128)S(1)} %get-tuple-element.21.z, f32[2,32,128]{2,1,0:T(8,128)S(1)} %collective-permute-done.ya_in, ...), custom_call_target="tpu_custom_call" | custom-call | flops 5242880 | bytes 4194304 | tf_op jit(solution)/shard_map/forward/pallas_call | solution.py:344
  11.3 17.7 %all_to_all.10.got = f32[16,7,8,128]{3,2,1,0:T(8,128)S(1)} all-to-all(f32[16,7,8,128]{3,2,1,0:T(8,128)S(1)} %get-tuple-element.31), channel_id=1, replica_groups=mesh['gx'=16,'gy'=4,'gz'=2] {'gx'}, dimensions={0} | all-to-all | bytes 917504 | tf_op jit(solution)/shard_map/all_to_all | solution.py:353
  28.9 0.2 reduced.1
  29.2 11.1 %all_to_all.11.ends = f32[16,2,8,128]{3,2,1,0:T(8,128)S(1)} all-to-all(f32[16,2,8,128]{3,2,1,0:T(8,128)S(1)} %reduced.1), channel_id=1, replica_groups=mesh['gx'=16,'gy'=4,'gz'=2] {'gx'}, dimensions={0} | all-to-all | bytes 262144 | tf_op jit(solution)/shard_map/all_to_all | solution.py:361
  40.3 1.4 %back.1 = f32[32,128,128]{2,1,0:T(8,128)} custom-call(f32[16,2,8,128]{3,2,1,0:T(8,128)S(1)} %all_to_all.11.ends, f32[32,128,128]{2,1,0:T(8,128)S(1)} %get-tuple-element.32.q_ref, f32[32,128,128]{2,1,0:T(8,128)S(1)} %get-tuple-element.27.t_ref, f32[32,128,128]{2,1,0:T(8,128)S(1)} %get-tuple-element.28.e_ref), custom_call_target="tpu_custom_call" | custom-call | flops 2097152 | bytes 4194304 | tf_op jit(solution)/shard_map/back/pallas_call | solution.py:362
Async XLA Ops:
  3.5 7.0 %collective-permute-start.2 = (f32[128,128]{1,0:T(8,128)S(1)}, f32[128,128]{1,0:T(8,128)S(1)}, u32[]{:S(2)}, u32[]{:S(2)}) collective-permute-start(f32[128,128]{1,0:T(8,128)S(1)} %get-tuple-element.21.z), channel_id=1, source_target_pairs={{0,1},{1,0},{2,3},{3,2},{4,5},{5,4},{6,7},{7,6},{8,9},{9,8},{10,11... | collective-permute-start | bytes 196616 | tf_op jit(solution)/shard_map/ppermute | solution.py:335
  3.6 6.9 %collective-permute-start = (f32[2,32,128]{2,1,0:T(8,128)S(1)}, f32[2,32,128]{2,1,0:T(8,128)S(1)}, u32[]{:S(2)}, u32[]{:S(2)}) collective-permute-start(f32[2,32,128]{2,1,0:T(8,128)S(1)} %get-tuple-element.19.ya), channel_id=1, source_target_pairs={{0,2},{2,0},{4,6},{6,4},{1,3},{3,1},{5,7},{7,5},{8,10},{10,8},{12,... | collective-permute-start | bytes 98312 | tf_op jit(solution)/shard_map/ppermute | solution.py:333
  3.7 6.8 %collective-permute-start.1 = (f32[2,32,128]{2,1,0:T(8,128)S(1)}, f32[2,32,128]{2,1,0:T(8,128)S(1)}, u32[]{:S(2)}, u32[]{:S(2)}) collective-permute-start(f32[2,32,128]{2,1,0:T(8,128)S(1)} %get-tuple-element.20.yb), channel_id=1, source_target_pairs={{0,1},{1,0},{2,4},{3,5},{4,2},{5,3},{6,7},{7,6},{8,9},{9,8},{10,12... | collective-permute-start | bytes 98312 | tf_op jit(solution)/shard_map/ppermute | solution.py:334
